TPU v7x, 512 devices: a whole 4x8x8 slice. The times are simulated.
512 devices in a mesh: dp: 8 (over y), cent: 64 (over x, z, core).
Axes of the slice: x: 4, y: 8, z: 8, core: 2. Of those that a mesh axis runs over, the one named last changes fastest.
Arguments:
- points: bfloat16 [12288, 1024], P('dp', 'cent'), may hold values from -8 to 8
- centroids: bfloat16 [65536, 1024], P('cent'), may hold values from -0.26 to 0.26
Outputs:
- new_centroids: bfloat16 [65536, 1024], P(('cent', 'dp'))
- counts: float32 [65536], P(('cent', 'dp'))
All inputs are finite; a program needn't handle non-finite values.
Results may differ from a plain program's by a relative error of at most 0.018.
Values may be sent and summed in bfloat16 or wider, within the bound.
No kernel may reach another device: no remote copies, remote signals or barrier semaphores. Data moves between devices by JAX's collectives and lax.ppermute only.
A program may use at most 64 MiB of HBM per device.

v0:
```python
import jax
import jax.numpy as jnp
from jax import lax
from jax.sharding import PartitionSpec as P

sharpness = 10.0
epsilon = 1e-12


def per_device(points, centroids):
    gathered = lax.all_gather(points, "cent", axis=1, tiled=True)
    center_norm = jnp.sum(jnp.square(centroids.astype(jnp.float32)), axis=1)
    product = lax.dot_general(
        gathered, centroids, (((1,), (1,)), ((), ())), preferred_element_type=jnp.float32
    )
    logits = sharpness * (product - 0.5 * center_norm[None, :])
    row_peak = lax.pmax(jnp.max(logits, axis=1), "cent")
    row_total = lax.psum(jnp.sum(jnp.exp(logits - row_peak[:, None]), axis=1), "cent")
    responsibility = (jnp.exp(logits - row_peak[:, None]) / row_total[:, None]).astype(jnp.bfloat16)
    part_sums = lax.dot_general(
        responsibility, gathered, (((0,), (0,)), ((), ())), preferred_element_type=jnp.float32
    )
    part_counts = jnp.sum(responsibility, axis=0, dtype=jnp.float32)
    sums, raw_counts = (
        lax.psum_scatter(
            part_sums.astype(jnp.bfloat16), "dp", scatter_dimension=0, tiled=True
        ).astype(jnp.float32),
        lax.psum_scatter(
            part_counts.astype(jnp.bfloat16), "dp", scatter_dimension=0, tiled=True
        ).astype(jnp.float32),
    )
    row_scale = lax.rsqrt(jnp.mean(sums * sums, axis=1, keepdims=True) + epsilon)
    fresh = (sums * row_scale).astype(jnp.bfloat16)
    factor = centroids.shape[0] * lax.axis_size("cent") / (points.shape[0] * lax.axis_size("dp"))
    return (fresh, raw_counts * factor)


def solution(mesh):
    in_specs = (P("dp", "cent"), P("cent", None))
    out_specs = (P(("cent", "dp"), None), P(("cent", "dp")))
    return jax.shard_map(
        per_device, mesh=mesh, in_specs=in_specs, out_specs=out_specs, check_vma=False
    )
```

profile of v0, /device:TPU:10, one launch (start us, length us, event | category | flops | bytes accessed | tf_op | source)
XLA Modules:
  0.0 424.0 jit_solution(16975972916574535115)
XLA Ops:
  7.2 0.0 all-gather.2.cloned.1.call-start
  7.2 0.7 all-gather.2.cloned.1.call-update
  7.9 0.0 reduce-scatter.2.cloned.1.call-start
  7.9 2.1 multiply_reduce_fusion
  10.0 89.1 %all-gather.2.cloned.1.call-done = bf16[1536,1024]{0,1:T(8,128)(2,1)} async-done(((bf16[1536,16]{0,1:T(8,128)(2,1)}), bf16[1536,1024]{0,1:T(8,128)(2,1)}) %all-gather.2.cloned.1.call-update) | async-done | bytes 3145744 | tf_op jit(solution)/shard_map/all_gather | solution.py:11
  99.2 8.6 %fusion = (f32[1536]{0:T(1024)S(1)}, f32[1536,1024]{0,1:T(8,128)}) fusion(f32[1024]{0:T(1024)S(1)} %broadcast_multiply_fusion, bf16[1024,1024]{1,0:T(8,128)(2,1)} %param.3, bf16[1536,1024]{0,1:T(8,128)(2,1)} %all-gather.2.cloned.1.call-done), kind=kOutput, calls=%fused_computation.3 | convolution fusion | flops 3225942528 | bytes 11544576 | tf_op jit(solution)/shard_map/dot_general | solution.py:13
  107.8 109.7 %pmax.7 = f32[1536]{0:T(1024)S(1)} all-reduce(f32[1536]{0:T(1024)S(1)} %get-tuple-element.4), channel_id=1, replica_groups=mesh['dp'=8,'cent'=64] {'cent'}, use_global_device_ids=true, to_apply=%region_2.0 | all-reduce | flops 1536 | bytes 12288 | tf_op jit(solution)/shard_map/pmax | solution.py:17
  217.5 4.1 fusion.1
  221.6 0.0 copy-start
  221.6 110.5 %psum.7 = f32[1536]{0:T(1024)S(1)} all-reduce(f32[1536]{0:T(1024)S(1)} %fusion.1), channel_id=1, replica_groups=mesh['dp'=8,'cent'=64] {'cent'}, use_global_device_ids=true, to_apply=%region_4.0 | all-reduce | flops 1536 | bytes 12288 | tf_op jit(solution)/shard_map/psum | solution.py:18
  332.1 3.9 fusion.5
  336.0 0.0 copy-done
  336.0 4.7 %convolution_convert_fusion = bf16[1024,1024]{1,0:T(8,128)(2,1)} fusion(bf16[1536,1024]{0,1:T(8,128)(2,1)S(1)} %get-tuple-element.3, bf16[1536,1024]{0,1:T(8,128)(2,1)S(1)} %copy-done), kind=kOutput, calls=%fused_computation.6 | convolution fusion | flops 3222274048 | bytes 8388608 | tf_op jit(solution)/shard_map/dot_general | solution.py:20
  340.8 0.0 reduce-scatter.2.cloned.1.call-update
  340.8 1.3 dynamic-slice
  342.7 15.7 %all-reduce = bf16[1024]{0:T(1024)(128)(2,1)S(1)} all-reduce(bf16[1024]{0:T(1024)(128)(2,1)S(1)} %get-tuple-element.2), channel_id=3, replica_groups=mesh['dp'=8,'cent'=64] {'dp'}, use_global_device_ids=true, to_apply=%region_8.0.clone | all-reduce | flops 1024 | bytes 4096
  358.5 0.6 fusion.4
  359.0 55.2 %reduce-scatter.2.cloned.1.call-done = bf16[128,1024]{1,0:T(8,128)(2,1)} async-done(((bf16[1024,1024]{1,0:T(8,128)(2,1)}), bf16[128,1024]{1,0:T(8,128)(2,1)}) %reduce-scatter.2.cloned.1.call-update) | async-done | bytes 262160 | tf_op jit(solution)/shard_map/reduce_scatter | solution.py:25
  414.3 1.1 fusion.2
  415.4 1.8 fusion.3
  (2 shorter events, 0.0 us)
Async XLA Ops:
  7.2 92.0 %all-gather.2.cloned.1.call-start = ((), (), s32[]{:S(2)}) async-start(), calls=%async_computation.1 | async-start | bytes 3194880 | tf_op jit(solution)/shard_map/all_gather | solution.py:11
  7.9 406.4 %reduce-scatter.2.cloned.1.call-start = ((), (), s32[]{:S(2)}) async-start(), calls=%async_computation.2 | async-start | bytes 2359296 | tf_op jit(solution)/shard_map/reduce_scatter | solution.py:25
  221.6 114.5 %copy-start = (bf16[1536,1024]{0,1:T(8,128)(2,1)S(1)}, bf16[1536,1024]{0,1:T(8,128)(2,1)}, u32[]{:S(2)}) copy-start(bf16[1536,1024]{0,1:T(8,128)(2,1)} %all-gather.2.cloned.1.call-done) | copy-start | bytes 9437188
Sparse Core Ops, SparseCore 0:
  11.3 87.7 all-gather.1
  340.9 73.3 reduce-scatter.1
where the time goes:
time: 424 us
  blocking collectives  236 us (56%)
  waiting for transfers between devices  145 us (34%)
  between operations  14.8 us (3%)
  other arithmetic  13.5 us (3%)
  matrix products  13.3 us (3%)
    psum x1, blocking collectives, per_device(): lax.psum(jnp.sum(jnp.exp(logits - row_peak[:, None]), axis=1), 'cent')  111 us
    pmax x1, blocking collectives, per_device(): row_peak = lax.pmax(jnp.max(logits, axis=1), 'cent')  110 us
    all_gather x1, waiting for transfers between devices, per_device(): gathered = lax.all_gather(points, 'cent', axis=1, tiled=True)  89.1 us
    reduce_scatter x1, waiting for transfers between devices, per_device(): lax.psum_scatter(part_sums.astype(jnp.bfloat16), 'dp', scatter_dimension=...  55.2 us
    unnamed x1, blocking collectives  15.7 us
    dot_general x1, matrix products, per_device(): lax.dot_general(gathered, centroids, (((1,), (1,)), ((), ())), preferred_...  8.59 us
  transfers between devices with their start and end apart: 2, of which 2 were waited for; matrix products, arithmetic and copies ran while one was open for 1% of the time, Pallas kernels for 0%

commit v1 on v0

v1 whole, which is shorter than its diff:
```python
import functools

import jax
import jax.numpy as jnp
from jax import lax
from jax.experimental import pallas as pl
from jax.experimental.pallas import tpu as pltpu
from jax.sharding import PartitionSpec as P

sharpness = 10.0
epsilon = 1e-12
lanes = 128
tile = 256
tall = 512
vmem = pl.BlockSpec(memory_space=pltpu.VMEM)
smem = pl.BlockSpec(memory_space=pltpu.SMEM)
hbm = pl.BlockSpec(memory_space=pltpu.HBM)


def limit(mib):
    return pltpu.CompilerParams(vmem_limit_bytes=mib << 20)


def logits_kernel(cent_ref, source_ref, points_ref, raised_ref, peak_ref, lse_ref, norm_ref, sems):
    n_cent, n_tok = raised_ref.shape
    row_blocks = [pl.ds(r, tall) for r in range(0, n_cent, tall)]
    token_blocks = [pl.ds(t, tile) for t in range(0, n_tok, tile)]
    copies = [
        pltpu.make_async_copy(source_ref.at[:, cols], points_ref.at[:, cols], sems.at[i])
        for i, cols in enumerate(token_blocks)
    ]
    for copy in copies:
        copy.start()
    for rows in row_blocks:
        entries = cent_ref[rows, :].astype(jnp.float32)
        half_norm = 0.5 * jnp.sum(entries * entries, axis=1, keepdims=True)
        norm_ref[rows, :] = jnp.broadcast_to(half_norm, (tall, lanes))
    peaks = []
    for step in range(len(token_blocks) + 1):
        if step < len(token_blocks):
            copies[step].wait()
        tops, totals = [], []
        for rows in row_blocks:
            if step < len(token_blocks):
                cols = token_blocks[step]
                product = jnp.dot(
                    cent_ref[rows, :], points_ref[:, cols], preferred_element_type=jnp.float32
                )
                logits = sharpness * (product - norm_ref[rows, :1])
                raised_ref[rows, cols] = logits
                tops.append(jnp.max(logits, axis=0, keepdims=True))
            if step > 0:
                cols = token_blocks[step - 1]
                raised = jnp.exp(raised_ref[rows, cols] - peaks[step - 1])
                raised_ref[rows, cols] = raised
                totals.append(jnp.sum(raised, axis=0, keepdims=True))
        if step < len(token_blocks):
            peaks.append(functools.reduce(jnp.maximum, tops))
            peak_ref[:, token_blocks[step]] = peaks[step]
        if step > 0:
            lse_ref[:, token_blocks[step - 1]] = peaks[step - 1] + jnp.log(sum(totals))


def local_softmax(centroids, points):
    n_cent, n_tok = centroids.shape[0], points.shape[1]
    row = jax.ShapeDtypeStruct((1, n_tok), jnp.float32)
    raised = jax.ShapeDtypeStruct((n_cent, n_tok), jnp.float32)
    return pl.pallas_call(
        logits_kernel,
        out_shape=(jax.ShapeDtypeStruct(points.shape, points.dtype), raised, row, row),
        in_specs=[vmem, hbm],
        out_specs=[vmem] * 4,
        scratch_shapes=[
            pltpu.VMEM((n_cent, lanes), jnp.float32), pltpu.SemaphoreType.DMA((n_tok // tile,)),
        ],
        compiler_params=limit(12),
        cost_estimate=pl.CostEstimate(
            flops=2 * centroids.size * n_tok, bytes_accessed=8 * n_cent * n_tok,
            transcendentals=n_cent * n_tok,
        ),
        name="local_softmax",
    )(centroids, points)


def sums_kernel(order, n_blocks, place_ref, lse_ref, *refs):
    halves, outs, resp_ref = (refs[0:3], refs[3:6]), refs[6:-1], refs[-1]
    share, width = outs[-1].shape
    depth = width - lanes
    far = len(outs) - len(order)
    cut = outs[0].shape[1]
    n_tok = refs[0].shape[1]

    def put(i, start, value):
        value = value.astype(jnp.bfloat16)
        if i > 0 or not far:
            outs[i + far][:, pl.ds(start, value.shape[1])] = value
        elif start < cut:
            outs[0][:, pl.ds(start, value.shape[1])] = value
        else:
            outs[1][:, pl.ds(start - cut, value.shape[1])] = value

    parts = lse_ref[...]
    top = jnp.max(parts, axis=0, keepdims=True)
    norm = top + jnp.log(jnp.sum(jnp.exp(parts - top), axis=0, keepdims=True))
    scales = [
        jnp.exp(half[1][...] - norm[:, h * n_tok:(h + 1) * n_tok]) for h, half in enumerate(halves)
    ]
    for i, d in enumerate(order):
        start = lax.rem(place_ref[0] + d + n_blocks, n_blocks) * share
        rows = pl.ds(pl.multiple_of(start, share), share)
        count = jnp.zeros((share, 1), jnp.float32)
        for h, half in enumerate(halves):
            resp = (half[0][rows, :] * scales[h]).astype(jnp.bfloat16)
            resp_ref[pl.ds(i * share, share), pl.ds(h * n_tok, n_tok)] = resp
            count += jnp.sum(resp.astype(jnp.float32), axis=1, keepdims=True)
        put(i, depth, jnp.broadcast_to(count, (share, lanes)))
    for i in range(0, len(order), tall // share):
        rows = min(tall, (len(order) - i) * share)
        for c in range(0, depth, tile):
            total = sum(
                lax.dot_general(
                    resp_ref[pl.ds(i * share, rows), pl.ds(h * n_tok, n_tok)],
                    half[2][pl.ds(c, tile), :],
                    (((1,), (1,)), ((), ())),
                    preferred_element_type=jnp.float32,
                )
                for h, half in enumerate(halves)
            )
            for k in range(rows // share):
                put(i + k, c, total[k * share:(k + 1) * share])


def weighted_sums(order, n_blocks, far, place, lse, halves):
    n_cent, n_tok = halves[0][0].shape
    depth = halves[0][2].shape[0]
    n = len(order)
    share, cut = n_cent // n_blocks, depth // 2
    widths = ((cut, depth + lanes - cut) if far else (depth + lanes,)) + (depth + lanes,) * (n - 1)
    return pl.pallas_call(
        functools.partial(sums_kernel, order, n_blocks),
        out_shape=tuple(jax.ShapeDtypeStruct((share, w), jnp.bfloat16) for w in widths),
        in_specs=[smem] + [vmem] * 7,
        out_specs=(vmem,) * len(widths),
        scratch_shapes=[pltpu.VMEM((n * share, 2 * n_tok), jnp.bfloat16)],
        compiler_params=limit(20),
        cost_estimate=pl.CostEstimate(
            flops=4 * n * share * n_tok * depth, bytes_accessed=16 * n * share * n_tok, transcendentals=0
        ),
        name="weighted_sums",
    )(place, lse, *halves[0], *halves[1])


def finish_kernel(factor, own_ref, down_ref, up_ref, fresh_ref, counts_ref):
    total = sum(ref[...].astype(jnp.float32) for ref in (own_ref, down_ref, up_ref))
    depth = fresh_ref.shape[1]
    sums = total[:, :depth]
    mean = jnp.sum(sums * sums, axis=1, keepdims=True) / depth
    fresh_ref[...] = (sums * lax.rsqrt(mean + epsilon)).astype(fresh_ref.dtype)
    counts_ref[...] = jnp.transpose(total[:, depth:] * factor)[:1]


def finish(own, down, up, factor):
    share, width = own.shape
    fresh, counts = pl.pallas_call(
        functools.partial(finish_kernel, factor),
        out_shape=(
            jax.ShapeDtypeStruct((share, width - lanes), jnp.bfloat16),
            jax.ShapeDtypeStruct((1, share), jnp.float32),
        ),
        in_specs=[vmem] * 3,
        out_specs=[vmem] * 2,
        compiler_params=limit(4),
        name="finish",
    )(own, down, up)
    return fresh, counts.reshape(share)


def core_swap(value):
    return lax.ppermute(value, "core", [(0, 1), (1, 0)])


def spread(value, axis):
    n = lax.psum(1, axis)
    return lax.all_to_all(jnp.broadcast_to(value[None], (n,) + value.shape), axis, 0, 0)


def gather_half(points):
    n_tok, cols = points.shape
    n_z, n_core = lax.axis_size("z"), lax.axis_size("core")
    part, rows = n_tok // n_core, points.T
    halves = jnp.stack([rows[:, c * part:(c + 1) * part] for c in range(n_core)])
    blocks = jnp.broadcast_to(halves[None], (n_z,) + halves.shape).reshape((n_z * n_core,) + halves.shape[1:])
    slab = lax.all_to_all(blocks, ("z", "core"), 0, 0).reshape(-1, n_tok // n_core)
    return spread(slab, "x").reshape(-1, n_tok // n_core)


def dp_shift(value, d):
    n = lax.axis_size("dp")
    return lax.ppermute(value, "dp", [((i + d) % n, i) for i in range(n)])


def ring_order(n):
    near = [s * d for d in range(n // 2 - 1, 0, -1) for s in (-1, 1)]
    return [n // 2] + near + [0]


def add(block, total, start):
    stop = start + total.shape[1]
    part = block[:, start:stop].astype(jnp.float32) + total.astype(jnp.float32)
    pieces = [block[:, :start], part.astype(block.dtype), block[:, stop:]]
    return jnp.concatenate([p for p in pieces if p.shape[1]], axis=1)


def ring_sum(far, near, make_rest):
    down, up = dp_shift(far[0], 1), dp_shift(far[1], -1)
    starts = 0, far[0].shape[1]
    rest = make_rest(up)
    while len(near) > 1:
        down = dp_shift(add(near[0], down, starts[0]), 1)
        up = dp_shift(add(near[1], up, starts[1]), -1)
        near, rest = (near[2:] or rest), (rest if near[2:] else ())
        starts = 0, 0
    return near[0], down, up


def per_device(points, centroids):
    n_dp = lax.axis_size("dp")
    n_cent = lax.axis_size("x") * lax.axis_size("z") * lax.axis_size("core")
    place = lax.axis_index("dp").astype(jnp.int32).reshape(1)
    points, place = lax.optimization_barrier((points, place))
    mine = gather_half(points)
    other = core_swap(mine)
    points_0, raised_0, peak_0, lse_0 = local_softmax(centroids, mine)
    points_1, raised_1, peak_1, lse_1 = local_softmax(centroids, other)
    here = jnp.concatenate([lse_0, lse_1], axis=1)
    there = core_swap(jnp.concatenate([lse_1, lse_0], axis=1))
    lse = spread(jnp.logaddexp(here, there)[0], ("x", "z"))
    halves = ((raised_0, peak_0, points_0), (raised_1, peak_1, points_1))
    order = ring_order(n_dp)
    first = weighted_sums(order[:3], n_dp, True, place, lse, halves)

    def make_rest(after):
        late, _ = lax.optimization_barrier((lse, after))
        return weighted_sums(order[3:], n_dp, False, place, late, halves)

    own, down, up = ring_sum(first[:2], first[2:], make_rest)
    factor = centroids.shape[0] * n_cent / (points.shape[0] * n_dp)
    return finish(own, down, up, factor)


def solution(mesh):
    n_dp = mesh.shape["dp"]
    split = (4, mesh.shape["cent"] // 8, 2)
    fine = jax.sharding.Mesh(mesh.devices.reshape((n_dp,) + split), ("dp", "x", "z", "core"))
    cent = ("x", "z", "core")
    in_specs = (P("dp", cent), P(cent, None))
    out_specs = (P(cent + ("dp",), None), P(cent + ("dp",)))
    return jax.shard_map(
        per_device, mesh=fine, in_specs=in_specs, out_specs=out_specs, check_vma=False
    )
```

time: 424 us -> 125 us (0.29)
  the two profiles are of different devices: /device:TPU:10 before, /device:TPU:64 now
where the time goes in v1:
time: 125 us; the launch traced here: 124 us
  blocking collectives  64.5 us (52%)
  starting transfers between devices  33.6 us (27%)
  waiting for transfers between devices  11.9 us (10%)
  Pallas kernels  11.7 us (9%)
    all_to_all x2, blocking collectives, spread(): lax.all_to_all(jnp.broadcast_to(value[None], (n,) + value.shape), axis, 0...  42.8 us
    ppermute x8, starting transfers between devices, dp_shift(): return lax.ppermute(value, 'dp', [((i + d) % n, i) for i in range(n)])  29.4 us
    all_to_all x1, blocking collectives, gather_half(): lax.all_to_all(blocks, ('z', 'core'), 0, 0).reshape(-1, n_tok // n_core)  21.7 us
    ppermute x8, waiting for transfers between devices, dp_shift(): return lax.ppermute(value, 'dp', [((i + d) % n, i) for i in range(n)])  11 us
    pallas_call x2, Pallas kernels, local_softmax(): pl.pallas_call(logits_kernel, out_shape=(jax.ShapeDtypeStruct(points.shap...  6.47 us
    pallas_call x2, Pallas kernels, weighted_sums(): pl.pallas_call(functools.partial(sums_kernel, order, n_blocks), out_shape...  4.33 us
    ppermute x2, starting transfers between devices, core_swap(): return lax.ppermute(value, 'core', [(0, 1), (1, 0)])  4.24 us
  transfers between devices with their start and end apart: 10, of which 7 were waited for; matrix products, arithmetic and copies ran while one was open for 0% of the time, Pallas kernels for 5%

profile of v1, /device:TPU:64, one launch (start us, length us, event | category | flops | bytes accessed | tf_op | source)
XLA Modules:
  0.0 124.0 jit_solution(17150604930270249156)
XLA Ops:
  0.6 0.8 slice_bitcast_fusion.1
  1.4 21.7 %all_to_all.18 = bf16[16,16,768]{2,1,0:T(8,128)(2,1)S(1)} all-to-all(bf16[16,16,768]{2,1,0:T(8,128)(2,1)S(1)} %bitcast.17), channel_id=1, replica_groups=mesh['dp'=8,'x'=4,'z'=8,'core'=2] {'z','core'}, dimensions={0} | all-to-all | bytes 786432 | tf_op jit(solution)/shard_map/all_to_all | solution.py:193
  23.1 0.1 broadcast_in_dim.20
  23.2 0.0 copy-start
  23.2 25.6 %all_to_all.19 = bf16[4,256,768]{2,1,0:T(8,128)(2,1)S(1)} all-to-all(bf16[4,256,768]{2,1,0:T(8,128)(2,1)S(1)} %broadcast_in_dim.20), channel_id=1, replica_groups=mesh['dp'=8,'x'=4,'z'=8,'core'=2] {'x'}, dimensions={0} | all-to-all | bytes 3145728 | tf_op jit(solution)/shard_map/all_to_all | solution.py:184
  48.8 1.9 %collective-permute-start = (bf16[1024,768]{1,0:T(8,128)(2,1)S(1)}, bf16[1024,768]{1,0:T(8,128)(2,1)S(1)}, u32[]{:S(2)}, u32[]{:S(2)}) collective-permute-start(bf16[1024,768]{1,0:T(8,128)(2,1)S(1)} %bitcast.15), channel_id=1, source_target_pairs={{0,1},{1,0},{2,3},{3,2},{4,5},{5,4},{6,7},{7,6},{8,9},{9,8},{10,11... | collective-permute-start | bytes 4718600 | tf_op jit(solution)/shard_map/ppermute | solution.py:179
  50.7 0.0 copy-done
  50.8 3.3 %local_softmax.2 = (bf16[1024,768]{1,0:T(8,128)(2,1)S(1)}, f32[1024,768]{1,0:T(8,128)S(1)}, f32[1,768]{1,0:T(1,128)S(1)}, f32[1,768]{1,0:T(1,128)S(1)}) custom-call(bf16[1024,1024]{1,0:T(8,128)(2,1)S(1)} %copy-done, bf16[1024,768]{1,0:T(8,128)(2,1)S(1)} %bitcast.16), custom_call_target="tpu_custom_call" | custom-call | flops 1610612736 | bytes 6291456 | tf_op jit(solution)/shard_map/local_softmax/pallas_call | solution.py:68
  54.0 0.1 collective-permute-done.source_ref
  54.1 3.2 %local_softmax.3 = (bf16[1024,768]{1,0:T(8,128)(2,1)S(1)}, f32[1024,768]{1,0:T(8,128)S(1)}, f32[1,768]{1,0:T(1,128)S(1)}, f32[1,768]{1,0:T(1,128)S(1)}) custom-call(bf16[1024,1024]{1,0:T(8,128)(2,1)S(1)} %copy-done, bf16[1024,768]{1,0:T(8,128)(2,1)S(1)} %collective-permute-done.source_ref), custom_call_target="tpu_custom_call" | custom-call | flops 1610612736 | bytes 6291456 | tf_op jit(solution)/shard_map/local_softmax/pallas_call | solution.py:68
  57.4 2.3 %collective-permute-start.1 = (f32[1,1536]{1,0:T(1,128)S(1)}, f32[1,1536]{1,0:T(1,128)S(1)}, u32[]{:S(2)}, u32[]{:S(2)}) collective-permute-start(f32[1,1536]{1,0:T(1,128)S(1)} %pad_maximum_fusion.3), channel_id=1, source_target_pairs={{0,1},{1,0},{2,3},{3,2},{4,5},{5,4},{6,7},{7,6},{8,9},{9,8},{10,11... | collective-permute-start | bytes 18440 | tf_op jit(solution)/shard_map/ppermute | solution.py:179
  59.7 0.8 collective-permute-done.1
  60.5 0.1 fusion
  60.6 0.1 broadcast_in_dim.21
  60.7 17.2 %all_to_all.20 = f32[32,1,1536]{2,1,0:T(1,128)S(1)} all-to-all(f32[32,1,1536]{2,1,0:T(1,128)S(1)} %broadcast_in_dim.21), channel_id=1, replica_groups=mesh['dp'=8,'x'=4,'z'=8,'core'=2] {'x','z'}, dimensions={0} | all-to-all | bytes 393216 | tf_op jit(solution)/shard_map/all_to_all | solution.py:184
  77.9 1.5 %weighted_sums.2 = (bf16[128,512]{1,0:T(8,128)(2,1)S(1)}, bf16[128,640]{1,0:T(8,128)(2,1)S(1)}, bf16[128,1152]{1,0:T(8,128)(2,1)S(1)}, bf16[128,1152]{1,0:T(8,128)(2,1)S(1)}) custom-call(s32[1]{0:T(128)} %bitcast.place_ref, f32[32,1536]{1,0:T(8,128)S(1)} %bitcast.13, f32[1024,768]{1,0:T(8,128)S(1)} %get-tuple-element.28.refs_0_, ...), custom_call_target="tpu_custom_call" | custom-call | flops 1207959552 | bytes 4718592 | tf_op jit(solution)/shard_map/weighted_sums/pallas_call | solution.py:139
  79.3 5.4 %collective-permute-start.3 = (bf16[128,512]{1,0:T(8,128)(2,1)S(1)}, bf16[128,512]{1,0:T(8,128)(2,1)S(1)}, u32[]{:S(2)}, u32[]{:S(2)}) collective-permute-start(bf16[128,512]{1,0:T(8,128)(2,1)S(1)} %get-tuple-element.40), channel_id=1, source_target_pairs={{64,0},{128,64},{192,128},{256,192},{320,256},{384,320},{448,384},... | collective-permute-start | bytes 393224 | tf_op jit(solution)/shard_map/ppermute | solution.py:199
  84.8 1.9 %collective-permute-start.2 = (bf16[128,640]{1,0:T(8,128)(2,1)S(1)}, bf16[128,640]{1,0:T(8,128)(2,1)S(1)}, u32[]{:S(2)}, u32[]{:S(2)}) collective-permute-start(bf16[128,640]{1,0:T(8,128)(2,1)S(1)} %get-tuple-element.34), channel_id=1, source_target_pairs={{448,0},{0,64},{64,128},{128,192},{192,256},{256,320},{320,384},{3... | collective-permute-start | bytes 491528 | tf_op jit(solution)/shard_map/ppermute | solution.py:199
  86.7 0.5 collective-permute-done.3
  87.3 5.6 %collective-permute-start.4 = (bf16[128,1152]{1,0:T(8,128)(2,1)S(1)}, bf16[128,1152]{1,0:T(8,128)(2,1)S(1)}, u32[]{:S(2)}, u32[]{:S(2)}) collective-permute-start(bf16[128,1152]{1,0:T(8,128)(2,1)S(1)} %pad_maximum_fusion), channel_id=1, source_target_pairs={{64,0},{128,64},{192,128},{256,192},{320,256},{384,320},{448,384},... | collective-permute-start | bytes 884744 | tf_op jit(solution)/shard_map/ppermute | solution.py:199
  92.9 0.3 collective-permute-done.2
  93.3 1.9 %collective-permute-start.7 = (bf16[128,1152]{1,0:T(8,128)(2,1)S(1)}, bf16[128,1152]{1,0:T(8,128)(2,1)S(1)}, u32[]{:S(2)}, u32[]{:S(2)}) collective-permute-start(bf16[128,1152]{1,0:T(8,128)(2,1)S(1)} %pad_maximum_fusion.1), channel_id=1, source_target_pairs={{448,0},{0,64},{64,128},{128,192},{192,256},{256,320},{320,384},{3... | collective-permute-start | bytes 884744 | tf_op jit(solution)/shard_map/ppermute | solution.py:199
  95.2 2.9 %weighted_sums.3 = (bf16[128,1152]{1,0:T(8,128)(2,1)S(1)}, bf16[128,1152]{1,0:T(8,128)(2,1)S(1)}, bf16[128,1152]{1,0:T(8,128)(2,1)S(1)}, bf16[128,1152]{1,0:T(8,128)(2,1)S(1)}, bf16[128,1152]{1,0:T(8,128)(2,1)S(1)}) custom-call(s32[1]{0:T(128)} %bitcast.place_ref, f32[32,1536]{1,0:T(8,128)S(1)} %bitcast.14, f32[1024,768]{1,0:T(8,128)S(1)} %get-tuple-element.28.refs_0_, ...), custom_call_target="tpu_custom_call" | custom-call | flops 2013265920 | bytes 7864320 | tf_op jit(solution)/shard_map/weighted_sums/pallas_call | solution.py:139
  98.1 0.0 collective-permute-done.4
  98.1 0.1 add_convert_fusion.3
  98.2 5.1 %collective-permute-start.5 = (bf16[128,1152]{1,0:T(8,128)(2,1)S(1)}, bf16[128,1152]{1,0:T(8,128)(2,1)S(1)}, u32[]{:S(2)}, u32[]{:S(2)}) collective-permute-start(bf16[128,1152]{1,0:T(8,128)(2,1)S(1)} %add_convert_fusion.3), channel_id=1, source_target_pairs={{64,0},{128,64},{192,128},{256,192},{320,256},{384,320},{448,384},... | collective-permute-start | bytes 884744 | tf_op jit(solution)/shard_map/ppermute | solution.py:199
  103.3 0.0 collective-permute-done.7
  103.3 0.1 add_convert_fusion.1
  103.4 1.9 %collective-permute-start.8 = (bf16[128,1152]{1,0:T(8,128)(2,1)S(1)}, bf16[128,1152]{1,0:T(8,128)(2,1)S(1)}, u32[]{:S(2)}, u32[]{:S(2)}) collective-permute-start(bf16[128,1152]{1,0:T(8,128)(2,1)S(1)} %add_convert_fusion.1), channel_id=1, source_target_pairs={{448,0},{0,64},{64,128},{128,192},{192,256},{256,320},{320,384},{3... | collective-permute-start | bytes 884744 | tf_op jit(solution)/shard_map/ppermute | solution.py:199
  105.3 2.2 %collective-permute-done.5 = bf16[128,1152]{1,0:T(8,128)(2,1)S(1)} collective-permute-done((bf16[128,1152]{1,0:T(8,128)(2,1)S(1)}, bf16[128,1152]{1,0:T(8,128)(2,1)S(1)}, u32[]{:S(2)}, u32[]{:S(2)}) %collective-permute-start.5) | collective-permute-done | bytes 294944 | tf_op jit(solution)/shard_map/ppermute | solution.py:199
  107.5 0.1 add_convert_fusion.2
  107.6 5.6 %collective-permute-start.6 = (bf16[128,1152]{1,0:T(8,128)(2,1)S(1)}, bf16[128,1152]{1,0:T(8,128)(2,1)S(1)}, u32[]{:S(2)}, u32[]{:S(2)}) collective-permute-start(bf16[128,1152]{1,0:T(8,128)(2,1)S(1)} %add_convert_fusion.2), channel_id=1, source_target_pairs={{64,0},{128,64},{192,128},{256,192},{320,256},{384,320},{448,384},... | collective-permute-start | bytes 884744 | tf_op jit(solution)/shard_map/ppermute | solution.py:199
  113.2 0.0 collective-permute-done.8
  113.2 0.1 add_convert_fusion
  113.3 1.9 %collective-permute-start.9 = (bf16[128,1152]{1,0:T(8,128)(2,1)S(1)}, bf16[128,1152]{1,0:T(8,128)(2,1)S(1)}, u32[]{:S(2)}, u32[]{:S(2)}) collective-permute-start(bf16[128,1152]{1,0:T(8,128)(2,1)S(1)} %add_convert_fusion), channel_id=1, source_target_pairs={{448,0},{0,64},{64,128},{128,192},{192,256},{256,320},{320,384},{3... | collective-permute-start | bytes 884744 | tf_op jit(solution)/shard_map/ppermute | solution.py:199
  115.2 2.2 %collective-permute-done.6.down_ref = bf16[128,1152]{1,0:T(8,128)(2,1)S(1)} collective-permute-done((bf16[128,1152]{1,0:T(8,128)(2,1)S(1)}, bf16[128,1152]{1,0:T(8,128)(2,1)S(1)}, u32[]{:S(2)}, u32[]{:S(2)}) %collective-permute-start.6) | collective-permute-done | bytes 294944 | tf_op jit(solution)/shard_map/ppermute | solution.py:199
  117.4 5.7 %collective-permute-done.9.up_ref = bf16[128,1152]{1,0:T(8,128)(2,1)S(1)} collective-permute-done((bf16[128,1152]{1,0:T(8,128)(2,1)S(1)}, bf16[128,1152]{1,0:T(8,128)(2,1)S(1)}, u32[]{:S(2)}, u32[]{:S(2)}) %collective-permute-start.9) | collective-permute-done | bytes 294944 | tf_op jit(solution)/shard_map/ppermute | solution.py:199
  123.1 0.9 finish.1
  (12 shorter events, 0.2 us)
Async XLA Ops:
  23.2 27.5 %copy-start = (bf16[1024,1024]{1,0:T(8,128)(2,1)S(1)}, bf16[1024,1024]{1,0:T(8,128)(2,1)}, u32[]{:S(2)}) copy-start(bf16[1024,1024]{1,0:T(8,128)(2,1)} %cent_ref.3) | copy-start | bytes 6291460
  48.8 5.3 %collective-permute-start = (bf16[1024,768]{1,0:T(8,128)(2,1)S(1)}, bf16[1024,768]{1,0:T(8,128)(2,1)S(1)}, u32[]{:S(2)}, u32[]{:S(2)}) collective-permute-start(bf16[1024,768]{1,0:T(8,128)(2,1)S(1)} %bitcast.15), channel_id=1, source_target_pairs={{0,1},{1,0},{2,3},{3,2},{4,5},{5,4},{6,7},{7,6},{8,9},{9,8},{10,11... | collective-permute-start | bytes 4718600 | tf_op jit(solution)/shard_map/ppermute | solution.py:179
  57.4 3.1 %collective-permute-start.1 = (f32[1,1536]{1,0:T(1,128)S(1)}, f32[1,1536]{1,0:T(1,128)S(1)}, u32[]{:S(2)}, u32[]{:S(2)}) collective-permute-start(f32[1,1536]{1,0:T(1,128)S(1)} %pad_maximum_fusion.3), channel_id=1, source_target_pairs={{0,1},{1,0},{2,3},{3,2},{4,5},{5,4},{6,7},{7,6},{8,9},{9,8},{10,11... | collective-permute-start | bytes 18440 | tf_op jit(solution)/shard_map/ppermute | solution.py:179
  79.3 7.9 %collective-permute-start.3 = (bf16[128,512]{1,0:T(8,128)(2,1)S(1)}, bf16[128,512]{1,0:T(8,128)(2,1)S(1)}, u32[]{:S(2)}, u32[]{:S(2)}) collective-permute-start(bf16[128,512]{1,0:T(8,128)(2,1)S(1)} %get-tuple-element.40), channel_id=1, source_target_pairs={{64,0},{128,64},{192,128},{256,192},{320,256},{384,320},{448,384},... | collective-permute-start | bytes 393224 | tf_op jit(solution)/shard_map/ppermute | solution.py:199
  84.8 8.4 %collective-permute-start.2 = (bf16[128,640]{1,0:T(8,128)(2,1)S(1)}, bf16[128,640]{1,0:T(8,128)(2,1)S(1)}, u32[]{:S(2)}, u32[]{:S(2)}) collective-permute-start(bf16[128,640]{1,0:T(8,128)(2,1)S(1)} %get-tuple-element.34), channel_id=1, source_target_pairs={{448,0},{0,64},{64,128},{128,192},{192,256},{256,320},{320,384},{3... | collective-permute-start | bytes 491528 | tf_op jit(solution)/shard_map/ppermute | solution.py:199
  87.3 10.8 %collective-permute-start.4 = (bf16[128,1152]{1,0:T(8,128)(2,1)S(1)}, bf16[128,1152]{1,0:T(8,128)(2,1)S(1)}, u32[]{:S(2)}, u32[]{:S(2)}) collective-permute-start(bf16[128,1152]{1,0:T(8,128)(2,1)S(1)} %pad_maximum_fusion), channel_id=1, source_target_pairs={{64,0},{128,64},{192,128},{256,192},{320,256},{384,320},{448,384},... | collective-permute-start | bytes 884744 | tf_op jit(solution)/shard_map/ppermute | solution.py:199
  93.3 10.0 %collective-permute-start.7 = (bf16[128,1152]{1,0:T(8,128)(2,1)S(1)}, bf16[128,1152]{1,0:T(8,128)(2,1)S(1)}, u32[]{:S(2)}, u32[]{:S(2)}) collective-permute-start(bf16[128,1152]{1,0:T(8,128)(2,1)S(1)} %pad_maximum_fusion.1), channel_id=1, source_target_pairs={{448,0},{0,64},{64,128},{128,192},{192,256},{256,320},{320,384},{3... | collective-permute-start | bytes 884744 | tf_op jit(solution)/shard_map/ppermute | solution.py:199
  98.2 9.4 %collective-permute-start.5 = (bf16[128,1152]{1,0:T(8,128)(2,1)S(1)}, bf16[128,1152]{1,0:T(8,128)(2,1)S(1)}, u32[]{:S(2)}, u32[]{:S(2)}) collective-permute-start(bf16[128,1152]{1,0:T(8,128)(2,1)S(1)} %add_convert_fusion.3), channel_id=1, source_target_pairs={{64,0},{128,64},{192,128},{256,192},{320,256},{384,320},{448,384},... | collective-permute-start | bytes 884744 | tf_op jit(solution)/shard_map/ppermute | solution.py:199
  103.4 9.8 %collective-permute-start.8 = (bf16[128,1152]{1,0:T(8,128)(2,1)S(1)}, bf16[128,1152]{1,0:T(8,128)(2,1)S(1)}, u32[]{:S(2)}, u32[]{:S(2)}) collective-permute-start(bf16[128,1152]{1,0:T(8,128)(2,1)S(1)} %add_convert_fusion.1), channel_id=1, source_target_pairs={{448,0},{0,64},{64,128},{128,192},{192,256},{256,320},{320,384},{3... | collective-permute-start | bytes 884744 | tf_op jit(solution)/shard_map/ppermute | solution.py:199
  107.6 9.8 %collective-permute-start.6 = (bf16[128,1152]{1,0:T(8,128)(2,1)S(1)}, bf16[128,1152]{1,0:T(8,128)(2,1)S(1)}, u32[]{:S(2)}, u32[]{:S(2)}) collective-permute-start(bf16[128,1152]{1,0:T(8,128)(2,1)S(1)} %add_convert_fusion.2), channel_id=1, source_target_pairs={{64,0},{128,64},{192,128},{256,192},{320,256},{384,320},{448,384},... | collective-permute-start | bytes 884744 | tf_op jit(solution)/shard_map/ppermute | solution.py:199
  113.3 9.8 %collective-permute-start.9 = (bf16[128,1152]{1,0:T(8,128)(2,1)S(1)}, bf16[128,1152]{1,0:T(8,128)(2,1)S(1)}, u32[]{:S(2)}, u32[]{:S(2)}) collective-permute-start(bf16[128,1152]{1,0:T(8,128)(2,1)S(1)} %add_convert_fusion), channel_id=1, source_target_pairs={{448,0},{0,64},{64,128},{128,192},{192,256},{256,320},{320,384},{3... | collective-permute-start | bytes 884744 | tf_op jit(solution)/shard_map/ppermute | solution.py:199

commit v2 on v1

--- a/solution.py
+++ b/solution.py
@@ -12,33 +12,31 @@
 lanes = 128
 tile = 256
 tall = 512
+count_rows = 16
 vmem = pl.BlockSpec(memory_space=pltpu.VMEM)
 smem = pl.BlockSpec(memory_space=pltpu.SMEM)
-hbm = pl.BlockSpec(memory_space=pltpu.HBM)
 
 
 def limit(mib):
     return pltpu.CompilerParams(vmem_limit_bytes=mib << 20)
 
 
-def logits_kernel(cent_ref, source_ref, points_ref, raised_ref, peak_ref, lse_ref, norm_ref, sems):
+def norms_kernel(cent_ref, points_ref, *refs):
+    norm_ref = refs[-1]
+    for r in range(0, cent_ref.shape[0], tall):
+        rows = pl.ds(r, tall)
+        entries = cent_ref[rows, :].astype(jnp.float32)
+        half_norm = 0.5 * jnp.sum(entries * entries, axis=1, keepdims=True)
+        norm_ref[rows, :] = jnp.broadcast_to(half_norm, (tall, lanes))
+    logits_kernel(cent_ref, points_ref, norm_ref, *refs[:-1])
+
+
+def logits_kernel(cent_ref, points_ref, norm_ref, raised_ref, peak_ref, lse_ref):
     n_cent, n_tok = raised_ref.shape
     row_blocks = [pl.ds(r, tall) for r in range(0, n_cent, tall)]
     token_blocks = [pl.ds(t, tile) for t in range(0, n_tok, tile)]
-    copies = [
-        pltpu.make_async_copy(source_ref.at[:, cols], points_ref.at[:, cols], sems.at[i])
-        for i, cols in enumerate(token_blocks)
-    ]
-    for copy in copies:
-        copy.start()
-    for rows in row_blocks:
-        entries = cent_ref[rows, :].astype(jnp.float32)
-        half_norm = 0.5 * jnp.sum(entries * entries, axis=1, keepdims=True)
-        norm_ref[rows, :] = jnp.broadcast_to(half_norm, (tall, lanes))
     peaks = []
     for step in range(len(token_blocks) + 1):
-        if step < len(token_blocks):
-            copies[step].wait()
         tops, totals = [], []
         for rows in row_blocks:
             if step < len(token_blocks):
@@ -61,43 +59,44 @@
             lse_ref[:, token_blocks[step - 1]] = peaks[step - 1] + jnp.log(sum(totals))
 
 
-def local_softmax(centroids, points):
+def local_softmax(centroids, points, norms=None):
     n_cent, n_tok = centroids.shape[0], points.shape[1]
     row = jax.ShapeDtypeStruct((1, n_tok), jnp.float32)
-    raised = jax.ShapeDtypeStruct((n_cent, n_tok), jnp.float32)
-    return pl.pallas_call(
-        logits_kernel,
-        out_shape=(jax.ShapeDtypeStruct(points.shape, points.dtype), raised, row, row),
-        in_specs=[vmem, hbm],
-        out_specs=[vmem] * 4,
-        scratch_shapes=[
-            pltpu.VMEM((n_cent, lanes), jnp.float32), pltpu.SemaphoreType.DMA((n_tok // tile,)),
-        ],
+    outs = (jax.ShapeDtypeStruct((n_cent, n_tok), jnp.float32), row, row)
+    if norms is None:
+        outs += (jax.ShapeDtypeStruct((n_cent, lanes), jnp.float32),)
+    operands = (centroids, points) + (() if norms is None else (norms,))
+    results = pl.pallas_call(
+        norms_kernel if norms is None else logits_kernel,
+        out_shape=outs,
+        in_specs=[vmem] * len(operands),
+        out_specs=[vmem] * len(outs),
         compiler_params=limit(12),
         cost_estimate=pl.CostEstimate(
             flops=2 * centroids.size * n_tok, bytes_accessed=8 * n_cent * n_tok,
             transcendentals=n_cent * n_tok,
         ),
         name="local_softmax",
-    )(centroids, points)
+    )(*operands)
+    return results if norms is None else (*results, norms)
 
 
 def sums_kernel(order, n_blocks, place_ref, lse_ref, *refs):
     halves, outs, resp_ref = (refs[0:3], refs[3:6]), refs[6:-1], refs[-1]
-    share, width = outs[-1].shape
-    depth = width - lanes
+    depth = halves[0][2].shape[0]
+    share = refs[0].shape[0] // n_blocks
+    n_tok = refs[0].shape[1]
     far = len(outs) - len(order)
-    cut = outs[0].shape[1]
-    n_tok = refs[0].shape[1]
+    cut = outs[0].shape[0]
 
     def put(i, start, value):
         value = value.astype(jnp.bfloat16)
         if i > 0 or not far:
-            outs[i + far][:, pl.ds(start, value.shape[1])] = value
+            outs[i + far][pl.ds(start, value.shape[0]), :] = value
         elif start < cut:
-            outs[0][:, pl.ds(start, value.shape[1])] = value
+            outs[0][pl.ds(start, value.shape[0]), :] = value
         else:
-            outs[1][:, pl.ds(start - cut, value.shape[1])] = value
+            outs[1][pl.ds(start - cut, value.shape[0]), :] = value
 
     parts = lse_ref[...]
     top = jnp.max(parts, axis=0, keepdims=True)
@@ -113,7 +112,7 @@
             resp = (half[0][rows, :] * scales[h]).astype(jnp.bfloat16)
             resp_ref[pl.ds(i * share, share), pl.ds(h * n_tok, n_tok)] = resp
             count += jnp.sum(resp.astype(jnp.float32), axis=1, keepdims=True)
-        put(i, depth, jnp.broadcast_to(count, (share, lanes)))
+        put(i, depth // lanes * share, jnp.transpose(jnp.broadcast_to(count, (share, lanes)))[:count_rows])
     for i in range(0, len(order), tall // share):
         rows = min(tall, (len(order) - i) * share)
         for c in range(0, depth, tile):
@@ -127,20 +126,22 @@
                 for h, half in enumerate(halves)
             )
             for k in range(rows // share):
-                put(i + k, c, total[k * share:(k + 1) * share])
+                for p in range(0, tile, lanes):
+                    put(i + k, (c + p) // lanes * share, total[k * share:(k + 1) * share, p:p + lanes])
 
 
 def weighted_sums(order, n_blocks, far, place, lse, halves):
     n_cent, n_tok = halves[0][0].shape
     depth = halves[0][2].shape[0]
     n = len(order)
-    share, cut = n_cent // n_blocks, depth // 2
-    widths = ((cut, depth + lanes - cut) if far else (depth + lanes,)) + (depth + lanes,) * (n - 1)
+    share = n_cent // n_blocks
+    height, cut = depth // lanes * share + count_rows, depth // lanes // 2 * share
+    heights = ((cut, height - cut) if far else (height,)) + (height,) * (n - 1)
     return pl.pallas_call(
         functools.partial(sums_kernel, order, n_blocks),
-        out_shape=tuple(jax.ShapeDtypeStruct((share, w), jnp.bfloat16) for w in widths),
+        out_shape=tuple(jax.ShapeDtypeStruct((h, lanes), jnp.bfloat16) for h in heights),
         in_specs=[smem] + [vmem] * 7,
-        out_specs=(vmem,) * len(widths),
+        out_specs=(vmem,) * len(heights),
         scratch_shapes=[pltpu.VMEM((n * share, 2 * n_tok), jnp.bfloat16)],
         compiler_params=limit(20),
         cost_estimate=pl.CostEstimate(
@@ -151,20 +152,25 @@
 
 
 def finish_kernel(factor, own_ref, down_ref, up_ref, fresh_ref, counts_ref):
-    total = sum(ref[...].astype(jnp.float32) for ref in (own_ref, down_ref, up_ref))
-    depth = fresh_ref.shape[1]
-    sums = total[:, :depth]
-    mean = jnp.sum(sums * sums, axis=1, keepdims=True) / depth
-    fresh_ref[...] = (sums * lax.rsqrt(mean + epsilon)).astype(fresh_ref.dtype)
-    counts_ref[...] = jnp.transpose(total[:, depth:] * factor)[:1]
-
-
-def finish(own, down, up, factor):
-    share, width = own.shape
+    share, depth = fresh_ref.shape
+
+    def total(start, size):
+        rows = pl.ds(start, size)
+        return sum(ref[rows, :].astype(jnp.float32) for ref in (own_ref, down_ref, up_ref))
+
+    pieces = [total(c // lanes * share, share) for c in range(0, depth, lanes)]
+    mean = jnp.sum(sum(piece * piece for piece in pieces), axis=1, keepdims=True) / depth
+    scale = lax.rsqrt(mean + epsilon)
+    for i, piece in enumerate(pieces):
+        fresh_ref[:, pl.ds(i * lanes, lanes)] = (piece * scale).astype(fresh_ref.dtype)
+    counts_ref[...] = total(depth // lanes * share, count_rows)[:1] * factor
+
+
+def finish(own, down, up, share, depth, factor):
     fresh, counts = pl.pallas_call(
         functools.partial(finish_kernel, factor),
         out_shape=(
-            jax.ShapeDtypeStruct((share, width - lanes), jnp.bfloat16),
+            jax.ShapeDtypeStruct((share, depth), jnp.bfloat16),
             jax.ShapeDtypeStruct((1, share), jnp.float32),
         ),
         in_specs=[vmem] * 3,
@@ -205,15 +211,15 @@
 
 
 def add(block, total, start):
-    stop = start + total.shape[1]
-    part = block[:, start:stop].astype(jnp.float32) + total.astype(jnp.float32)
-    pieces = [block[:, :start], part.astype(block.dtype), block[:, stop:]]
-    return jnp.concatenate([p for p in pieces if p.shape[1]], axis=1)
+    stop = start + total.shape[0]
+    part = block[start:stop].astype(jnp.float32) + total.astype(jnp.float32)
+    pieces = [block[:start], part.astype(block.dtype), block[stop:]]
+    return jnp.concatenate([p for p in pieces if p.shape[0]], axis=0)
 
 
 def ring_sum(far, near, make_rest):
     down, up = dp_shift(far[0], 1), dp_shift(far[1], -1)
-    starts = 0, far[0].shape[1]
+    starts = 0, far[0].shape[0]
     rest = make_rest(up)
     while len(near) > 1:
         down = dp_shift(add(near[0], down, starts[0]), 1)
@@ -230,12 +236,12 @@
     points, place = lax.optimization_barrier((points, place))
     mine = gather_half(points)
     other = core_swap(mine)
-    points_0, raised_0, peak_0, lse_0 = local_softmax(centroids, mine)
-    points_1, raised_1, peak_1, lse_1 = local_softmax(centroids, other)
+    raised_0, peak_0, lse_0, norms = local_softmax(centroids, mine)
+    raised_1, peak_1, lse_1, _ = local_softmax(centroids, other, norms)
     here = jnp.concatenate([lse_0, lse_1], axis=1)
     there = core_swap(jnp.concatenate([lse_1, lse_0], axis=1))
     lse = spread(jnp.logaddexp(here, there)[0], ("x", "z"))
-    halves = ((raised_0, peak_0, points_0), (raised_1, peak_1, points_1))
+    halves = ((raised_0, peak_0, mine), (raised_1, peak_1, other))
     order = ring_order(n_dp)
     first = weighted_sums(order[:3], n_dp, True, place, lse, halves)
 
@@ -245,7 +251,7 @@
 
     own, down, up = ring_sum(first[:2], first[2:], make_rest)
     factor = centroids.shape[0] * n_cent / (points.shape[0] * n_dp)
-    return finish(own, down, up, factor)
+    return finish(own, down, up, centroids.shape[0] // n_dp, centroids.shape[1], factor)
 
 
 def solution(mesh):

time: 125 us -> 123 us (0.984)
  the two profiles are of different devices: /device:TPU:64 before, /device:TPU:2 now
where the time goes in v2:
time: 123 us; the launch traced here: 122 us
  blocking collectives  64.4 us (52%)
  starting transfers between devices  33.4 us (27%)
  waiting for transfers between devices  11.5 us (9%)
  Pallas kernels  10.4 us (8%)
    all_to_all x2, blocking collectives, spread(): lax.all_to_all(jnp.broadcast_to(value[None], (n,) + value.shape), axis, 0...  40.5 us
    ppermute x8, starting transfers between devices, dp_shift(): return lax.ppermute(value, 'dp', [((i + d) % n, i) for i in range(n)])  29.4 us
    all_to_all x1, blocking collectives, gather_half(): lax.all_to_all(blocks, ('z', 'core'), 0, 0).reshape(-1, n_tok // n_core)  23.9 us
    ppermute x8, waiting for transfers between devices, dp_shift(): return lax.ppermute(value, 'dp', [((i + d) % n, i) for i in range(n)])  10 us
    pallas_call x2, Pallas kernels, local_softmax(): pl.pallas_call(norms_kernel if norms is None else logits_kernel, out_shap...  5.22 us
    pallas_call x2, Pallas kernels, weighted_sums(): pl.pallas_call(functools.partial(sums_kernel, order, n_blocks), out_shape...  4.25 us
    ppermute x2, starting transfers between devices, core_swap(): return lax.ppermute(value, 'core', [(0, 1), (1, 0)])  4.06 us
  transfers between devices with their start and end apart: 10, of which 6 were waited for; matrix products, arithmetic and copies ran while one was open for 0% of the time, Pallas kernels for 5%

profile of v2, /device:TPU:2, one launch (start us, length us, event | category | flops | bytes accessed | tf_op | source)
XLA Modules:
  0.0 122.1 jit_solution(10225039670838272994)
XLA Ops:
  0.6 0.8 slice_bitcast_fusion.1
  1.4 23.9 %all_to_all.18 = bf16[16,16,768]{2,1,0:T(8,128)(2,1)S(1)} all-to-all(bf16[16,16,768]{2,1,0:T(8,128)(2,1)S(1)} %bitcast.19), channel_id=1, replica_groups=mesh['dp'=8,'x'=4,'z'=8,'core'=2] {'z','core'}, dimensions={0} | all-to-all | bytes 786432 | tf_op jit(solution)/shard_map/all_to_all | solution.py:199
  25.3 0.0 copy-start
  25.3 0.1 broadcast_in_dim.20
  25.5 25.4 %all_to_all.19 = bf16[4,256,768]{2,1,0:T(8,128)(2,1)S(1)} all-to-all(bf16[4,256,768]{2,1,0:T(8,128)(2,1)S(1)} %broadcast_in_dim.20), channel_id=1, replica_groups=mesh['dp'=8,'x'=4,'z'=8,'core'=2] {'x'}, dimensions={0} | all-to-all | bytes 3145728 | tf_op jit(solution)/shard_map/all_to_all | solution.py:190
  50.9 2.0 %collective-permute-start = (bf16[1024,768]{1,0:T(8,128)(2,1)S(1)}, bf16[1024,768]{1,0:T(8,128)(2,1)S(1)}, u32[]{:S(2)}, u32[]{:S(2)}) collective-permute-start(bf16[1024,768]{1,0:T(8,128)(2,1)S(1)} %bitcast.13), channel_id=1, source_target_pairs={{0,1},{1,0},{2,3},{3,2},{4,5},{5,4},{6,7},{7,6},{8,9},{9,8},{10,11... | collective-permute-start | bytes 4718600 | tf_op jit(solution)/shard_map/ppermute | solution.py:185
  52.9 0.0 copy-done
  52.9 2.8 %local_softmax.2 = (f32[1024,768]{1,0:T(8,128)S(1)}, f32[1,768]{1,0:T(1,128)S(1)}, f32[1,768]{1,0:T(1,128)S(1)}, f32[1024,128]{1,0:T(8,128)S(1)}) custom-call(bf16[1024,1024]{1,0:T(8,128)(2,1)S(1)} %copy-done, bf16[1024,768]{1,0:T(8,128)(2,1)S(1)} %bitcast.14), custom_call_target="tpu_custom_call" | custom-call | flops 1610612736 | bytes 6291456 | tf_op jit(solution)/shard_map/local_softmax/pallas_call | solution.py:69
  55.6 0.5 collective-permute-done.points_ref.refs_5_
  56.1 2.5 %local_softmax.3 = (f32[1024,768]{1,0:T(8,128)S(1)}, f32[1,768]{1,0:T(1,128)S(1)}, f32[1,768]{1,0:T(1,128)S(1)}) custom-call(bf16[1024,1024]{1,0:T(8,128)(2,1)S(1)} %copy-done, bf16[1024,768]{1,0:T(8,128)(2,1)S(1)} %collective-permute-done.points_ref.refs_5_, f32[1024,128]{1,0:T(8,128)S(1)} %get-tuple-element.26.norm_ref), custom_call_target="tpu_custom_call" | custom-call | flops 1610612736 | bytes 6291456 | tf_op jit(solution)/shard_map/local_softmax/pallas_call | solution.py:69
  58.6 2.1 %collective-permute-start.1 = (f32[1,1536]{1,0:T(1,128)S(1)}, f32[1,1536]{1,0:T(1,128)S(1)}, u32[]{:S(2)}, u32[]{:S(2)}) collective-permute-start(f32[1,1536]{1,0:T(1,128)S(1)} %pad_maximum_fusion.3), channel_id=1, source_target_pairs={{0,1},{1,0},{2,3},{3,2},{4,5},{5,4},{6,7},{7,6},{8,9},{9,8},{10,11... | collective-permute-start | bytes 18440 | tf_op jit(solution)/shard_map/ppermute | solution.py:185
  60.7 1.0 collective-permute-done.1
  61.7 0.1 fusion
  61.7 0.1 broadcast_in_dim.21
  61.9 15.1 %all_to_all.20 = f32[32,1,1536]{2,1,0:T(1,128)S(1)} all-to-all(f32[32,1,1536]{2,1,0:T(1,128)S(1)} %broadcast_in_dim.21), channel_id=1, replica_groups=mesh['dp'=8,'x'=4,'z'=8,'core'=2] {'x','z'}, dimensions={0} | all-to-all | bytes 393216 | tf_op jit(solution)/shard_map/all_to_all | solution.py:190
  76.9 1.4 %weighted_sums.2 = (bf16[512,128]{1,0:T(8,128)(2,1)S(1)}, bf16[528,128]{1,0:T(8,128)(2,1)S(1)}, bf16[1040,128]{1,0:T(8,128)(2,1)S(1)}, bf16[1040,128]{1,0:T(8,128)(2,1)S(1)}) custom-call(s32[1]{0:T(128)} %bitcast.place_ref, f32[32,1536]{1,0:T(8,128)S(1)} %bitcast.17, f32[1024,768]{1,0:T(8,128)S(1)} %get-tuple-element.28.refs_0_, ...), custom_call_target="tpu_custom_call" | custom-call | flops 1207959552 | bytes 4718592 | tf_op jit(solution)/shard_map/weighted_sums/pallas_call | solution.py:140
  78.4 5.4 %collective-permute-start.3 = (bf16[512,128]{1,0:T(8,128)(2,1)S(1)}, bf16[512,128]{1,0:T(8,128)(2,1)S(1)}, u32[]{:S(2)}, u32[]{:S(2)}) collective-permute-start(bf16[512,128]{1,0:T(8,128)(2,1)S(1)} %get-tuple-element.38), channel_id=1, source_target_pairs={{64,0},{128,64},{192,128},{256,192},{320,256},{384,320},{448,384},... | collective-permute-start | bytes 393224 | tf_op jit(solution)/shard_map/ppermute | solution.py:205
  83.8 1.9 %collective-permute-start.2 = (bf16[528,128]{1,0:T(8,128)(2,1)S(1)}, bf16[528,128]{1,0:T(8,128)(2,1)S(1)}, u32[]{:S(2)}, u32[]{:S(2)}) collective-permute-start(bf16[528,128]{1,0:T(8,128)(2,1)S(1)} %get-tuple-element.32), channel_id=1, source_target_pairs={{448,0},{0,64},{64,128},{128,192},{192,256},{256,320},{320,384},{3... | collective-permute-start | bytes 405512 | tf_op jit(solution)/shard_map/ppermute | solution.py:205
  85.7 0.5 collective-permute-done.3
  86.3 5.6 %collective-permute-start.4 = (bf16[1040,128]{1,0:T(8,128)(2,1)S(1)}, bf16[1040,128]{1,0:T(8,128)(2,1)S(1)}, u32[]{:S(2)}, u32[]{:S(2)}) collective-permute-start(bf16[1040,128]{1,0:T(8,128)(2,1)S(1)} %pad_maximum_fusion), channel_id=1, source_target_pairs={{64,0},{128,64},{192,128},{256,192},{320,256},{384,320},{448,384},... | collective-permute-start | bytes 798728 | tf_op jit(solution)/shard_map/ppermute | solution.py:205
  91.9 0.0 collective-permute-done.2
  92.0 1.9 %collective-permute-start.7 = (bf16[1040,128]{1,0:T(8,128)(2,1)S(1)}, bf16[1040,128]{1,0:T(8,128)(2,1)S(1)}, u32[]{:S(2)}, u32[]{:S(2)}) collective-permute-start(bf16[1040,128]{1,0:T(8,128)(2,1)S(1)} %pad_maximum_fusion.1), channel_id=1, source_target_pairs={{448,0},{0,64},{64,128},{128,192},{192,256},{256,320},{320,384},{3... | collective-permute-start | bytes 798728 | tf_op jit(solution)/shard_map/ppermute | solution.py:205
  93.9 2.8 %weighted_sums.3 = (bf16[1040,128]{1,0:T(8,128)(2,1)S(1)}, bf16[1040,128]{1,0:T(8,128)(2,1)S(1)}, bf16[1040,128]{1,0:T(8,128)(2,1)S(1)}, bf16[1040,128]{1,0:T(8,128)(2,1)S(1)}, bf16[1040,128]{1,0:T(8,128)(2,1)S(1)}) custom-call(s32[1]{0:T(128)} %bitcast.place_ref, f32[32,1536]{1,0:T(8,128)S(1)} %bitcast.18, f32[1024,768]{1,0:T(8,128)S(1)} %get-tuple-element.28.refs_0_, ...), custom_call_target="tpu_custom_call" | custom-call | flops 2013265920 | bytes 7864320 | tf_op jit(solution)/shard_map/weighted_sums/pallas_call | solution.py:140
  96.7 0.0 collective-permute-done.4
  96.8 0.1 add_convert_fusion.3
  96.8 5.1 %collective-permute-start.5 = (bf16[1040,128]{1,0:T(8,128)(2,1)S(1)}, bf16[1040,128]{1,0:T(8,128)(2,1)S(1)}, u32[]{:S(2)}, u32[]{:S(2)}) collective-permute-start(bf16[1040,128]{1,0:T(8,128)(2,1)S(1)} %add_convert_fusion.3), channel_id=1, source_target_pairs={{64,0},{128,64},{192,128},{256,192},{320,256},{384,320},{448,384},... | collective-permute-start | bytes 798728 | tf_op jit(solution)/shard_map/ppermute | solution.py:205
  102.0 0.0 collective-permute-done.7
  102.0 0.1 add_convert_fusion.1
  102.1 1.9 %collective-permute-start.8 = (bf16[1040,128]{1,0:T(8,128)(2,1)S(1)}, bf16[1040,128]{1,0:T(8,128)(2,1)S(1)}, u32[]{:S(2)}, u32[]{:S(2)}) collective-permute-start(bf16[1040,128]{1,0:T(8,128)(2,1)S(1)} %add_convert_fusion.1), channel_id=1, source_target_pairs={{448,0},{0,64},{64,128},{128,192},{192,256},{256,320},{320,384},{3... | collective-permute-start | bytes 798728 | tf_op jit(solution)/shard_map/ppermute | solution.py:205
  104.0 1.9 %collective-permute-done.5 = bf16[1040,128]{1,0:T(8,128)(2,1)S(1)} collective-permute-done((bf16[1040,128]{1,0:T(8,128)(2,1)S(1)}, bf16[1040,128]{1,0:T(8,128)(2,1)S(1)}, u32[]{:S(2)}, u32[]{:S(2)}) %collective-permute-start.5) | collective-permute-done | bytes 266272 | tf_op jit(solution)/shard_map/ppermute | solution.py:205
  105.9 0.1 add_convert_fusion.2
  106.0 5.6 %collective-permute-start.6 = (bf16[1040,128]{1,0:T(8,128)(2,1)S(1)}, bf16[1040,128]{1,0:T(8,128)(2,1)S(1)}, u32[]{:S(2)}, u32[]{:S(2)}) collective-permute-start(bf16[1040,128]{1,0:T(8,128)(2,1)S(1)} %add_convert_fusion.2), channel_id=1, source_target_pairs={{64,0},{128,64},{192,128},{256,192},{320,256},{384,320},{448,384},... | collective-permute-start | bytes 798728 | tf_op jit(solution)/shard_map/ppermute | solution.py:205
  111.6 0.0 collective-permute-done.8
  111.6 0.1 add_convert_fusion
  111.7 1.9 %collective-permute-start.9 = (bf16[1040,128]{1,0:T(8,128)(2,1)S(1)}, bf16[1040,128]{1,0:T(8,128)(2,1)S(1)}, u32[]{:S(2)}, u32[]{:S(2)}) collective-permute-start(bf16[1040,128]{1,0:T(8,128)(2,1)S(1)} %add_convert_fusion), channel_id=1, source_target_pairs={{448,0},{0,64},{64,128},{128,192},{192,256},{256,320},{320,384},{3... | collective-permute-start | bytes 798728 | tf_op jit(solution)/shard_map/ppermute | solution.py:205
  113.6 1.9 %collective-permute-done.6.down_ref = bf16[1040,128]{1,0:T(8,128)(2,1)S(1)} collective-permute-done((bf16[1040,128]{1,0:T(8,128)(2,1)S(1)}, bf16[1040,128]{1,0:T(8,128)(2,1)S(1)}, u32[]{:S(2)}, u32[]{:S(2)}) %collective-permute-start.6) | collective-permute-done | bytes 266272 | tf_op jit(solution)/shard_map/ppermute | solution.py:205
  115.5 5.7 %collective-permute-done.9.up_ref = bf16[1040,128]{1,0:T(8,128)(2,1)S(1)} collective-permute-done((bf16[1040,128]{1,0:T(8,128)(2,1)S(1)}, bf16[1040,128]{1,0:T(8,128)(2,1)S(1)}, u32[]{:S(2)}, u32[]{:S(2)}) %collective-permute-start.9) | collective-permute-done | bytes 266272 | tf_op jit(solution)/shard_map/ppermute | solution.py:205
  121.2 0.9 finish.1
  (12 shorter events, 0.2 us)
Async XLA Ops:
  25.3 27.5 %copy-start = (bf16[1024,1024]{1,0:T(8,128)(2,1)S(1)}, bf16[1024,1024]{1,0:T(8,128)(2,1)}, u32[]{:S(2)}) copy-start(bf16[1024,1024]{1,0:T(8,128)(2,1)} %cent_ref.3) | copy-start | bytes 6291460
  50.9 5.3 %collective-permute-start = (bf16[1024,768]{1,0:T(8,128)(2,1)S(1)}, bf16[1024,768]{1,0:T(8,128)(2,1)S(1)}, u32[]{:S(2)}, u32[]{:S(2)}) collective-permute-start(bf16[1024,768]{1,0:T(8,128)(2,1)S(1)} %bitcast.13), channel_id=1, source_target_pairs={{0,1},{1,0},{2,3},{3,2},{4,5},{5,4},{6,7},{7,6},{8,9},{9,8},{10,11... | collective-permute-start | bytes 4718600 | tf_op jit(solution)/shard_map/ppermute | solution.py:185
  58.6 3.1 %collective-permute-start.1 = (f32[1,1536]{1,0:T(1,128)S(1)}, f32[1,1536]{1,0:T(1,128)S(1)}, u32[]{:S(2)}, u32[]{:S(2)}) collective-permute-start(f32[1,1536]{1,0:T(1,128)S(1)} %pad_maximum_fusion.3), channel_id=1, source_target_pairs={{0,1},{1,0},{2,3},{3,2},{4,5},{5,4},{6,7},{7,6},{8,9},{9,8},{10,11... | collective-permute-start | bytes 18440 | tf_op jit(solution)/shard_map/ppermute | solution.py:185
  78.4 7.9 %collective-permute-start.3 = (bf16[512,128]{1,0:T(8,128)(2,1)S(1)}, bf16[512,128]{1,0:T(8,128)(2,1)S(1)}, u32[]{:S(2)}, u32[]{:S(2)}) collective-permute-start(bf16[512,128]{1,0:T(8,128)(2,1)S(1)} %get-tuple-element.38), channel_id=1, source_target_pairs={{64,0},{128,64},{192,128},{256,192},{320,256},{384,320},{448,384},... | collective-permute-start | bytes 393224 | tf_op jit(solution)/shard_map/ppermute | solution.py:205
  83.8 8.1 %collective-permute-start.2 = (bf16[528,128]{1,0:T(8,128)(2,1)S(1)}, bf16[528,128]{1,0:T(8,128)(2,1)S(1)}, u32[]{:S(2)}, u32[]{:S(2)}) collective-permute-start(bf16[528,128]{1,0:T(8,128)(2,1)S(1)} %get-tuple-element.32), channel_id=1, source_target_pairs={{448,0},{0,64},{64,128},{128,192},{192,256},{256,320},{320,384},{3... | collective-permute-start | bytes 405512 | tf_op jit(solution)/shard_map/ppermute | solution.py:205
  86.3 10.4 %collective-permute-start.4 = (bf16[1040,128]{1,0:T(8,128)(2,1)S(1)}, bf16[1040,128]{1,0:T(8,128)(2,1)S(1)}, u32[]{:S(2)}, u32[]{:S(2)}) collective-permute-start(bf16[1040,128]{1,0:T(8,128)(2,1)S(1)} %pad_maximum_fusion), channel_id=1, source_target_pairs={{64,0},{128,64},{192,128},{256,192},{320,256},{384,320},{448,384},... | collective-permute-start | bytes 798728 | tf_op jit(solution)/shard_map/ppermute | solution.py:205
  92.0 10.0 %collective-permute-start.7 = (bf16[1040,128]{1,0:T(8,128)(2,1)S(1)}, bf16[1040,128]{1,0:T(8,128)(2,1)S(1)}, u32[]{:S(2)}, u32[]{:S(2)}) collective-permute-start(bf16[1040,128]{1,0:T(8,128)(2,1)S(1)} %pad_maximum_fusion.1), channel_id=1, source_target_pairs={{448,0},{0,64},{64,128},{128,192},{192,256},{256,320},{320,384},{3... | collective-permute-start | bytes 798728 | tf_op jit(solution)/shard_map/ppermute | solution.py:205
  96.8 9.1 %collective-permute-start.5 = (bf16[1040,128]{1,0:T(8,128)(2,1)S(1)}, bf16[1040,128]{1,0:T(8,128)(2,1)S(1)}, u32[]{:S(2)}, u32[]{:S(2)}) collective-permute-start(bf16[1040,128]{1,0:T(8,128)(2,1)S(1)} %add_convert_fusion.3), channel_id=1, source_target_pairs={{64,0},{128,64},{192,128},{256,192},{320,256},{384,320},{448,384},... | collective-permute-start | bytes 798728 | tf_op jit(solution)/shard_map/ppermute | solution.py:205
  102.1 9.5 %collective-permute-start.8 = (bf16[1040,128]{1,0:T(8,128)(2,1)S(1)}, bf16[1040,128]{1,0:T(8,128)(2,1)S(1)}, u32[]{:S(2)}, u32[]{:S(2)}) collective-permute-start(bf16[1040,128]{1,0:T(8,128)(2,1)S(1)} %add_convert_fusion.1), channel_id=1, source_target_pairs={{448,0},{0,64},{64,128},{128,192},{192,256},{256,320},{320,384},{3... | collective-permute-start | bytes 798728 | tf_op jit(solution)/shard_map/ppermute | solution.py:205
  106.0 9.5 %collective-permute-start.6 = (bf16[1040,128]{1,0:T(8,128)(2,1)S(1)}, bf16[1040,128]{1,0:T(8,128)(2,1)S(1)}, u32[]{:S(2)}, u32[]{:S(2)}) collective-permute-start(bf16[1040,128]{1,0:T(8,128)(2,1)S(1)} %add_convert_fusion.2), channel_id=1, source_target_pairs={{64,0},{128,64},{192,128},{256,192},{320,256},{384,320},{448,384},... | collective-permute-start | bytes 798728 | tf_op jit(solution)/shard_map/ppermute | solution.py:205
  111.7 9.5 %collective-permute-start.9 = (bf16[1040,128]{1,0:T(8,128)(2,1)S(1)}, bf16[1040,128]{1,0:T(8,128)(2,1)S(1)}, u32[]{:S(2)}, u32[]{:S(2)}) collective-permute-start(bf16[1040,128]{1,0:T(8,128)(2,1)S(1)} %add_convert_fusion), channel_id=1, source_target_pairs={{448,0},{0,64},{64,128},{128,192},{192,256},{256,320},{320,384},{3... | collective-permute-start | bytes 798728 | tf_op jit(solution)/shard_map/ppermute | solution.py:205

commit v3 on v2

--- a/solution.py
+++ b/solution.py
@@ -220,11 +220,11 @@
 def ring_sum(far, near, make_rest):
     down, up = dp_shift(far[0], 1), dp_shift(far[1], -1)
     starts = 0, far[0].shape[0]
-    rest = make_rest(up)
     while len(near) > 1:
+        rest = make_rest(up) if len(near) == 2 else near[2:]
         down = dp_shift(add(near[0], down, starts[0]), 1)
         up = dp_shift(add(near[1], up, starts[1]), -1)
-        near, rest = (near[2:] or rest), (rest if near[2:] else ())
+        near = rest
         starts = 0, 0
     return near[0], down, up
 
@@ -244,10 +244,11 @@
     halves = ((raised_0, peak_0, mine), (raised_1, peak_1, other))
     order = ring_order(n_dp)
     first = weighted_sums(order[:3], n_dp, True, place, lse, halves)
+    rounds = [order[i:i + 2] for i in range(3, n_dp - 3, 2)] + [order[-3:]]
 
     def make_rest(after):
         late, _ = lax.optimization_barrier((lse, after))
-        return weighted_sums(order[3:], n_dp, False, place, late, halves)
+        return weighted_sums(rounds.pop(0), n_dp, False, place, late, halves)
 
     own, down, up = ring_sum(first[:2], first[2:], make_rest)
     factor = centroids.shape[0] * n_cent / (points.shape[0] * n_dp)

time: 123 us -> 123 us (level)
    pallas_call x2 -> x3, Pallas kernels: 4.25 us -> 3.98 us  [weighted_sums(): pl.pallas_call(functools.partial(sums_kernel, order, n_blocks), out_shape...]
  transfers between devices with their start and end apart: 10 -> 10, of which waited for: 6 -> 8; matrix products, arithmetic and copies ran while one was open for 0% -> 0% of each run, Pallas kernels for 5% -> 4%
where the time goes in v3:
time: 123 us; the launch traced here: 122 us
  blocking collectives  64.4 us (52%)
  starting transfers between devices  33.9 us (28%)
  waiting for transfers between devices  11.2 us (9%)
  Pallas kernels  10.1 us (8%)
    all_to_all x2, blocking collectives, spread(): lax.all_to_all(jnp.broadcast_to(value[None], (n,) + value.shape), axis, 0...  40.5 us
    ppermute x8, starting transfers between devices, dp_shift(): return lax.ppermute(value, 'dp', [((i + d) % n, i) for i in range(n)])  29.8 us
    all_to_all x1, blocking collectives, gather_half(): lax.all_to_all(blocks, ('z', 'core'), 0, 0).reshape(-1, n_tok // n_core)  23.9 us
    ppermute x8, waiting for transfers between devices, dp_shift(): return lax.ppermute(value, 'dp', [((i + d) % n, i) for i in range(n)])  9.7 us
    pallas_call x2, Pallas kernels, local_softmax(): pl.pallas_call(norms_kernel if norms is None else logits_kernel, out_shap...  5.16 us
    ppermute x2, starting transfers between devices, core_swap(): return lax.ppermute(value, 'core', [(0, 1), (1, 0)])  4.06 us
    pallas_call x3, Pallas kernels, weighted_sums(): pl.pallas_call(functools.partial(sums_kernel, order, n_blocks), out_shape...  3.98 us
  transfers between devices with their start and end apart: 10, of which 8 were waited for; matrix products, arithmetic and copies ran while one was open for 0% of the time, Pallas kernels for 4%

profile of v3, /device:TPU:2, one launch (start us, length us, event | category | flops | bytes accessed | tf_op | source)
XLA Modules:
  0.0 122.0 jit_solution(18077778648132730061)
XLA Ops:
  0.6 0.8 slice_bitcast_fusion.1
  1.4 23.9 %all_to_all.18 = bf16[16,16,768]{2,1,0:T(8,128)(2,1)S(1)} all-to-all(bf16[16,16,768]{2,1,0:T(8,128)(2,1)S(1)} %bitcast.21), channel_id=1, replica_groups=mesh['dp'=8,'x'=4,'z'=8,'core'=2] {'z','core'}, dimensions={0} | all-to-all | bytes 786432 | tf_op jit(solution)/shard_map/all_to_all | solution.py:199
  25.3 0.0 copy-start
  25.3 0.1 broadcast_in_dim.20
  25.5 25.4 %all_to_all.19 = bf16[4,256,768]{2,1,0:T(8,128)(2,1)S(1)} all-to-all(bf16[4,256,768]{2,1,0:T(8,128)(2,1)S(1)} %broadcast_in_dim.20), channel_id=1, replica_groups=mesh['dp'=8,'x'=4,'z'=8,'core'=2] {'x'}, dimensions={0} | all-to-all | bytes 3145728 | tf_op jit(solution)/shard_map/all_to_all | solution.py:190
  50.9 2.0 %collective-permute-start = (bf16[1024,768]{1,0:T(8,128)(2,1)S(1)}, bf16[1024,768]{1,0:T(8,128)(2,1)S(1)}, u32[]{:S(2)}, u32[]{:S(2)}) collective-permute-start(bf16[1024,768]{1,0:T(8,128)(2,1)S(1)} %bitcast.13), channel_id=1, source_target_pairs={{0,1},{1,0},{2,3},{3,2},{4,5},{5,4},{6,7},{7,6},{8,9},{9,8},{10,11... | collective-permute-start | bytes 4718600 | tf_op jit(solution)/shard_map/ppermute | solution.py:185
  52.9 0.0 copy-done
  52.9 2.7 %local_softmax.2 = (f32[1024,768]{1,0:T(8,128)S(1)}, f32[1,768]{1,0:T(1,128)S(1)}, f32[1,768]{1,0:T(1,128)S(1)}, f32[1024,128]{1,0:T(8,128)S(1)}) custom-call(bf16[1024,1024]{1,0:T(8,128)(2,1)S(1)} %copy-done, bf16[1024,768]{1,0:T(8,128)(2,1)S(1)} %bitcast.14), custom_call_target="tpu_custom_call" | custom-call | flops 1610612736 | bytes 6291456 | tf_op jit(solution)/shard_map/local_softmax/pallas_call | solution.py:69
  55.6 0.5 collective-permute-done.points_ref.refs_5_
  56.1 2.5 %local_softmax.3 = (f32[1024,768]{1,0:T(8,128)S(1)}, f32[1,768]{1,0:T(1,128)S(1)}, f32[1,768]{1,0:T(1,128)S(1)}) custom-call(bf16[1024,1024]{1,0:T(8,128)(2,1)S(1)} %copy-done, bf16[1024,768]{1,0:T(8,128)(2,1)S(1)} %collective-permute-done.points_ref.refs_5_, f32[1024,128]{1,0:T(8,128)S(1)} %get-tuple-element.27.norm_ref), custom_call_target="tpu_custom_call" | custom-call | flops 1610612736 | bytes 6291456 | tf_op jit(solution)/shard_map/local_softmax/pallas_call | solution.py:69
  58.6 2.1 %collective-permute-start.1 = (f32[1,1536]{1,0:T(1,128)S(1)}, f32[1,1536]{1,0:T(1,128)S(1)}, u32[]{:S(2)}, u32[]{:S(2)}) collective-permute-start(f32[1,1536]{1,0:T(1,128)S(1)} %pad_maximum_fusion.3), channel_id=1, source_target_pairs={{0,1},{1,0},{2,3},{3,2},{4,5},{5,4},{6,7},{7,6},{8,9},{9,8},{10,11... | collective-permute-start | bytes 18440 | tf_op jit(solution)/shard_map/ppermute | solution.py:185
  60.7 1.0 collective-permute-done.1
  61.7 0.1 fusion
  61.7 0.1 broadcast_in_dim.21
  61.8 15.1 %all_to_all.20 = f32[32,1,1536]{2,1,0:T(1,128)S(1)} all-to-all(f32[32,1,1536]{2,1,0:T(1,128)S(1)} %broadcast_in_dim.21), channel_id=1, replica_groups=mesh['dp'=8,'x'=4,'z'=8,'core'=2] {'x','z'}, dimensions={0} | all-to-all | bytes 393216 | tf_op jit(solution)/shard_map/all_to_all | solution.py:190
  76.9 1.5 %weighted_sums.3 = (bf16[512,128]{1,0:T(8,128)(2,1)S(1)}, bf16[528,128]{1,0:T(8,128)(2,1)S(1)}, bf16[1040,128]{1,0:T(8,128)(2,1)S(1)}, bf16[1040,128]{1,0:T(8,128)(2,1)S(1)}) custom-call(s32[1]{0:T(128)} %bitcast.place_ref, f32[32,1536]{1,0:T(8,128)S(1)} %bitcast.18, f32[1024,768]{1,0:T(8,128)S(1)} %get-tuple-element.29.refs_0_, ...), custom_call_target="tpu_custom_call" | custom-call | flops 1207959552 | bytes 4718592 | tf_op jit(solution)/shard_map/weighted_sums/pallas_call | solution.py:140
  78.4 5.4 %collective-permute-start.4 = (bf16[512,128]{1,0:T(8,128)(2,1)S(1)}, bf16[512,128]{1,0:T(8,128)(2,1)S(1)}, u32[]{:S(2)}, u32[]{:S(2)}) collective-permute-start(bf16[512,128]{1,0:T(8,128)(2,1)S(1)} %get-tuple-element.41), channel_id=1, source_target_pairs={{64,0},{128,64},{192,128},{256,192},{320,256},{384,320},{448,384},... | collective-permute-start | bytes 393224 | tf_op jit(solution)/shard_map/ppermute | solution.py:205
  83.8 1.9 %collective-permute-start.2 = (bf16[528,128]{1,0:T(8,128)(2,1)S(1)}, bf16[528,128]{1,0:T(8,128)(2,1)S(1)}, u32[]{:S(2)}, u32[]{:S(2)}) collective-permute-start(bf16[528,128]{1,0:T(8,128)(2,1)S(1)} %get-tuple-element.34), channel_id=1, source_target_pairs={{448,0},{0,64},{64,128},{128,192},{192,256},{256,320},{320,384},{3... | collective-permute-start | bytes 405512 | tf_op jit(solution)/shard_map/ppermute | solution.py:205
  85.8 0.5 collective-permute-done.4
  86.4 5.6 %collective-permute-start.5 = (bf16[1040,128]{1,0:T(8,128)(2,1)S(1)}, bf16[1040,128]{1,0:T(8,128)(2,1)S(1)}, u32[]{:S(2)}, u32[]{:S(2)}) collective-permute-start(bf16[1040,128]{1,0:T(8,128)(2,1)S(1)} %pad_maximum_fusion.1), channel_id=1, source_target_pairs={{64,0},{128,64},{192,128},{256,192},{320,256},{384,320},{448,384},... | collective-permute-start | bytes 798728 | tf_op jit(solution)/shard_map/ppermute | solution.py:205
  91.9 0.0 collective-permute-done.2
  92.0 1.9 %collective-permute-start.3 = (bf16[1040,128]{1,0:T(8,128)(2,1)S(1)}, bf16[1040,128]{1,0:T(8,128)(2,1)S(1)}, u32[]{:S(2)}, u32[]{:S(2)}) collective-permute-start(bf16[1040,128]{1,0:T(8,128)(2,1)S(1)} %pad_maximum_fusion), channel_id=1, source_target_pairs={{448,0},{0,64},{64,128},{128,192},{192,256},{256,320},{320,384},{3... | collective-permute-start | bytes 798728 | tf_op jit(solution)/shard_map/ppermute | solution.py:205
  93.9 1.0 weighted_sums.5
  95.0 0.8 collective-permute-done.5
  95.8 0.1 add_convert_fusion.3
  95.9 5.6 %collective-permute-start.6 = (bf16[1040,128]{1,0:T(8,128)(2,1)S(1)}, bf16[1040,128]{1,0:T(8,128)(2,1)S(1)}, u32[]{:S(2)}, u32[]{:S(2)}) collective-permute-start(bf16[1040,128]{1,0:T(8,128)(2,1)S(1)} %add_convert_fusion.3), channel_id=1, source_target_pairs={{64,0},{128,64},{192,128},{256,192},{320,256},{384,320},{448,384},... | collective-permute-start | bytes 798728 | tf_op jit(solution)/shard_map/ppermute | solution.py:205
  101.5 0.0 collective-permute-done.3
  101.5 0.1 add_convert_fusion.1
  101.6 1.9 %collective-permute-start.8 = (bf16[1040,128]{1,0:T(8,128)(2,1)S(1)}, bf16[1040,128]{1,0:T(8,128)(2,1)S(1)}, u32[]{:S(2)}, u32[]{:S(2)}) collective-permute-start(bf16[1040,128]{1,0:T(8,128)(2,1)S(1)} %add_convert_fusion.1), channel_id=1, source_target_pairs={{448,0},{0,64},{64,128},{128,192},{192,256},{256,320},{320,384},{3... | collective-permute-start | bytes 798728 | tf_op jit(solution)/shard_map/ppermute | solution.py:205
  103.5 1.5 %weighted_sums.4 = (bf16[1040,128]{1,0:T(8,128)(2,1)S(1)}, bf16[1040,128]{1,0:T(8,128)(2,1)S(1)}, bf16[1040,128]{1,0:T(8,128)(2,1)S(1)}) custom-call(s32[1]{0:T(128)} %bitcast.place_ref, f32[32,1536]{1,0:T(8,128)S(1)} %bitcast.20, f32[1024,768]{1,0:T(8,128)S(1)} %get-tuple-element.29.refs_0_, f32[1,768]{1,0:T(1,128)S(1)} %get-tuple-element.30.refs_1_, ...), custom_call_target="tpu_custom_call" | custom-call | flops 1207959552 | bytes 4718592 | tf_op jit(solution)/shard_map/weighted_sums/pallas_call | solution.py:140
  105.0 0.4 collective-permute-done.6
  105.4 0.1 add_convert_fusion.2
  105.5 5.6 %collective-permute-start.7 = (bf16[1040,128]{1,0:T(8,128)(2,1)S(1)}, bf16[1040,128]{1,0:T(8,128)(2,1)S(1)}, u32[]{:S(2)}, u32[]{:S(2)}) collective-permute-start(bf16[1040,128]{1,0:T(8,128)(2,1)S(1)} %add_convert_fusion.2), channel_id=1, source_target_pairs={{64,0},{128,64},{192,128},{256,192},{320,256},{384,320},{448,384},... | collective-permute-start | bytes 798728 | tf_op jit(solution)/shard_map/ppermute | solution.py:205
  111.1 0.3 collective-permute-done.8
  111.4 0.1 add_convert_fusion
  111.5 1.9 %collective-permute-start.9 = (bf16[1040,128]{1,0:T(8,128)(2,1)S(1)}, bf16[1040,128]{1,0:T(8,128)(2,1)S(1)}, u32[]{:S(2)}, u32[]{:S(2)}) collective-permute-start(bf16[1040,128]{1,0:T(8,128)(2,1)S(1)} %add_convert_fusion), channel_id=1, source_target_pairs={{448,0},{0,64},{64,128},{128,192},{192,256},{256,320},{320,384},{3... | collective-permute-start | bytes 798728 | tf_op jit(solution)/shard_map/ppermute | solution.py:205
  113.4 1.6 %collective-permute-done.7.down_ref = bf16[1040,128]{1,0:T(8,128)(2,1)S(1)} collective-permute-done((bf16[1040,128]{1,0:T(8,128)(2,1)S(1)}, bf16[1040,128]{1,0:T(8,128)(2,1)S(1)}, u32[]{:S(2)}, u32[]{:S(2)}) %collective-permute-start.7) | collective-permute-done | bytes 266272 | tf_op jit(solution)/shard_map/ppermute | solution.py:205
  115.1 6.0 %collective-permute-done.9.up_ref = bf16[1040,128]{1,0:T(8,128)(2,1)S(1)} collective-permute-done((bf16[1040,128]{1,0:T(8,128)(2,1)S(1)}, bf16[1040,128]{1,0:T(8,128)(2,1)S(1)}, u32[]{:S(2)}, u32[]{:S(2)}) %collective-permute-start.9) | collective-permute-done | bytes 266272 | tf_op jit(solution)/shard_map/ppermute | solution.py:205
  121.0 0.9 finish.1
  (12 shorter events, 0.2 us)
Async XLA Ops:
  25.3 27.5 %copy-start = (bf16[1024,1024]{1,0:T(8,128)(2,1)S(1)}, bf16[1024,1024]{1,0:T(8,128)(2,1)}, u32[]{:S(2)}) copy-start(bf16[1024,1024]{1,0:T(8,128)(2,1)} %cent_ref.3) | copy-start | bytes 6291460
  50.9 5.3 %collective-permute-start = (bf16[1024,768]{1,0:T(8,128)(2,1)S(1)}, bf16[1024,768]{1,0:T(8,128)(2,1)S(1)}, u32[]{:S(2)}, u32[]{:S(2)}) collective-permute-start(bf16[1024,768]{1,0:T(8,128)(2,1)S(1)} %bitcast.13), channel_id=1, source_target_pairs={{0,1},{1,0},{2,3},{3,2},{4,5},{5,4},{6,7},{7,6},{8,9},{9,8},{10,11... | collective-permute-start | bytes 4718600 | tf_op jit(solution)/shard_map/ppermute | solution.py:185
  58.6 3.1 %collective-permute-start.1 = (f32[1,1536]{1,0:T(1,128)S(1)}, f32[1,1536]{1,0:T(1,128)S(1)}, u32[]{:S(2)}, u32[]{:S(2)}) collective-permute-start(f32[1,1536]{1,0:T(1,128)S(1)} %pad_maximum_fusion.3), channel_id=1, source_target_pairs={{0,1},{1,0},{2,3},{3,2},{4,5},{5,4},{6,7},{7,6},{8,9},{9,8},{10,11... | collective-permute-start | bytes 18440 | tf_op jit(solution)/shard_map/ppermute | solution.py:185
  78.4 7.9 %collective-permute-start.4 = (bf16[512,128]{1,0:T(8,128)(2,1)S(1)}, bf16[512,128]{1,0:T(8,128)(2,1)S(1)}, u32[]{:S(2)}, u32[]{:S(2)}) collective-permute-start(bf16[512,128]{1,0:T(8,128)(2,1)S(1)} %get-tuple-element.41), channel_id=1, source_target_pairs={{64,0},{128,64},{192,128},{256,192},{320,256},{384,320},{448,384},... | collective-permute-start | bytes 393224 | tf_op jit(solution)/shard_map/ppermute | solution.py:205
  83.8 8.1 %collective-permute-start.2 = (bf16[528,128]{1,0:T(8,128)(2,1)S(1)}, bf16[528,128]{1,0:T(8,128)(2,1)S(1)}, u32[]{:S(2)}, u32[]{:S(2)}) collective-permute-start(bf16[528,128]{1,0:T(8,128)(2,1)S(1)} %get-tuple-element.34), channel_id=1, source_target_pairs={{448,0},{0,64},{64,128},{128,192},{192,256},{256,320},{320,384},{3... | collective-permute-start | bytes 405512 | tf_op jit(solution)/shard_map/ppermute | solution.py:205
  86.4 9.5 %collective-permute-start.5 = (bf16[1040,128]{1,0:T(8,128)(2,1)S(1)}, bf16[1040,128]{1,0:T(8,128)(2,1)S(1)}, u32[]{:S(2)}, u32[]{:S(2)}) collective-permute-start(bf16[1040,128]{1,0:T(8,128)(2,1)S(1)} %pad_maximum_fusion.1), channel_id=1, source_target_pairs={{64,0},{128,64},{192,128},{256,192},{320,256},{384,320},{448,384},... | collective-permute-start | bytes 798728 | tf_op jit(solution)/shard_map/ppermute | solution.py:205
  92.0 9.5 %collective-permute-start.3 = (bf16[1040,128]{1,0:T(8,128)(2,1)S(1)}, bf16[1040,128]{1,0:T(8,128)(2,1)S(1)}, u32[]{:S(2)}, u32[]{:S(2)}) collective-permute-start(bf16[1040,128]{1,0:T(8,128)(2,1)S(1)} %pad_maximum_fusion), channel_id=1, source_target_pairs={{448,0},{0,64},{64,128},{128,192},{192,256},{256,320},{320,384},{3... | collective-permute-start | bytes 798728 | tf_op jit(solution)/shard_map/ppermute | solution.py:205
  95.9 9.5 %collective-permute-start.6 = (bf16[1040,128]{1,0:T(8,128)(2,1)S(1)}, bf16[1040,128]{1,0:T(8,128)(2,1)S(1)}, u32[]{:S(2)}, u32[]{:S(2)}) collective-permute-start(bf16[1040,128]{1,0:T(8,128)(2,1)S(1)} %add_convert_fusion.3), channel_id=1, source_target_pairs={{64,0},{128,64},{192,128},{256,192},{320,256},{384,320},{448,384},... | collective-permute-start | bytes 798728 | tf_op jit(solution)/shard_map/ppermute | solution.py:205
  101.6 9.8 %collective-permute-start.8 = (bf16[1040,128]{1,0:T(8,128)(2,1)S(1)}, bf16[1040,128]{1,0:T(8,128)(2,1)S(1)}, u32[]{:S(2)}, u32[]{:S(2)}) collective-permute-start(bf16[1040,128]{1,0:T(8,128)(2,1)S(1)} %add_convert_fusion.1), channel_id=1, source_target_pairs={{448,0},{0,64},{64,128},{128,192},{192,256},{256,320},{320,384},{3... | collective-permute-start | bytes 798728 | tf_op jit(solution)/shard_map/ppermute | solution.py:205
  105.5 9.5 %collective-permute-start.7 = (bf16[1040,128]{1,0:T(8,128)(2,1)S(1)}, bf16[1040,128]{1,0:T(8,128)(2,1)S(1)}, u32[]{:S(2)}, u32[]{:S(2)}) collective-permute-start(bf16[1040,128]{1,0:T(8,128)(2,1)S(1)} %add_convert_fusion.2), channel_id=1, source_target_pairs={{64,0},{128,64},{192,128},{256,192},{320,256},{384,320},{448,384},... | collective-permute-start | bytes 798728 | tf_op jit(solution)/shard_map/ppermute | solution.py:205
  111.5 9.5 %collective-permute-start.9 = (bf16[1040,128]{1,0:T(8,128)(2,1)S(1)}, bf16[1040,128]{1,0:T(8,128)(2,1)S(1)}, u32[]{:S(2)}, u32[]{:S(2)}) collective-permute-start(bf16[1040,128]{1,0:T(8,128)(2,1)S(1)} %add_convert_fusion), channel_id=1, source_target_pairs={{448,0},{0,64},{64,128},{128,192},{192,256},{256,320},{320,384},{3... | collective-permute-start | bytes 798728 | tf_op jit(solution)/shard_map/ppermute | solution.py:205

commit v4 on v3

--- a/solution.py
+++ b/solution.py
@@ -217,11 +217,12 @@
     return jnp.concatenate([p for p in pieces if p.shape[0]], axis=0)
 
 
-def ring_sum(far, near, make_rest):
+def ring_sum(far, make_near):
     down, up = dp_shift(far[0], 1), dp_shift(far[1], -1)
     starts = 0, far[0].shape[0]
+    near = make_near(far[0])
     while len(near) > 1:
-        rest = make_rest(up) if len(near) == 2 else near[2:]
+        rest = make_near(up) if len(near) == 2 else near[2:]
         down = dp_shift(add(near[0], down, starts[0]), 1)
         up = dp_shift(add(near[1], up, starts[1]), -1)
         near = rest
@@ -243,14 +244,14 @@
     lse = spread(jnp.logaddexp(here, there)[0], ("x", "z"))
     halves = ((raised_0, peak_0, mine), (raised_1, peak_1, other))
     order = ring_order(n_dp)
-    first = weighted_sums(order[:3], n_dp, True, place, lse, halves)
-    rounds = [order[i:i + 2] for i in range(3, n_dp - 3, 2)] + [order[-3:]]
-
-    def make_rest(after):
+    far = weighted_sums(order[:1], n_dp, True, place, lse, halves)
+    rounds = [order[i:i + 2] for i in range(1, n_dp - 3, 2)] + [order[-3:]]
+
+    def make_near(after):
         late, _ = lax.optimization_barrier((lse, after))
         return weighted_sums(rounds.pop(0), n_dp, False, place, late, halves)
 
-    own, down, up = ring_sum(first[:2], first[2:], make_rest)
+    own, down, up = ring_sum(far, make_near)
     factor = centroids.shape[0] * n_cent / (points.shape[0] * n_dp)
     return finish(own, down, up, centroids.shape[0] // n_dp, centroids.shape[1], factor)
 

time: 123 us -> 122 us (level)
  the two profiles are of different devices: /device:TPU:2 before, /device:TPU:64 now
where the time goes in v4:
time: 122 us
  blocking collectives  64.3 us (53%)
  starting transfers between devices  33.3 us (27%)
  waiting for transfers between devices  10.9 us (9%)
  Pallas kernels  10.8 us (9%)
    all_to_all x2, blocking collectives, spread(): lax.all_to_all(jnp.broadcast_to(value[None], (n,) + value.shape), axis, 0...  42.6 us
    ppermute x8, starting transfers between devices, dp_shift(): return lax.ppermute(value, 'dp', [((i + d) % n, i) for i in range(n)])  29.4 us
    all_to_all x1, blocking collectives, gather_half(): lax.all_to_all(blocks, ('z', 'core'), 0, 0).reshape(-1, n_tok // n_core)  21.7 us
    ppermute x8, waiting for transfers between devices, dp_shift(): return lax.ppermute(value, 'dp', [((i + d) % n, i) for i in range(n)])  9.28 us
    pallas_call x2, Pallas kernels, local_softmax(): pl.pallas_call(norms_kernel if norms is None else logits_kernel, out_shap...  5.17 us
    pallas_call x4, Pallas kernels, weighted_sums(): pl.pallas_call(functools.partial(sums_kernel, order, n_blocks), out_shape...  4.71 us
    ppermute x2, starting transfers between devices, core_swap(): return lax.ppermute(value, 'core', [(0, 1), (1, 0)])  3.95 us
  transfers between devices with their start and end apart: 10, of which 6 were waited for; matrix products, arithmetic and copies ran while one was open for 0% of the time, Pallas kernels for 5%

profile of v4, /device:TPU:64, one launch (start us, length us, event | category | flops | bytes accessed | tf_op | source)
XLA Modules:
  0.0 121.8 jit_solution(1688518003193220440)
XLA Ops:
  0.6 0.8 slice_bitcast_fusion.1
  1.4 21.7 %all_to_all.18 = bf16[16,16,768]{2,1,0:T(8,128)(2,1)S(1)} all-to-all(bf16[16,16,768]{2,1,0:T(8,128)(2,1)S(1)} %bitcast.23), channel_id=1, replica_groups=mesh['dp'=8,'x'=4,'z'=8,'core'=2] {'z','core'}, dimensions={0} | all-to-all | bytes 786432 | tf_op jit(solution)/shard_map/all_to_all | solution.py:199
  23.1 0.0 copy-start
  23.1 0.1 broadcast_in_dim.20
  23.2 25.6 %all_to_all.19 = bf16[4,256,768]{2,1,0:T(8,128)(2,1)S(1)} all-to-all(bf16[4,256,768]{2,1,0:T(8,128)(2,1)S(1)} %broadcast_in_dim.20), channel_id=1, replica_groups=mesh['dp'=8,'x'=4,'z'=8,'core'=2] {'x'}, dimensions={0} | all-to-all | bytes 3145728 | tf_op jit(solution)/shard_map/all_to_all | solution.py:190
  48.8 1.9 %collective-permute-start = (bf16[1024,768]{1,0:T(8,128)(2,1)S(1)}, bf16[1024,768]{1,0:T(8,128)(2,1)S(1)}, u32[]{:S(2)}, u32[]{:S(2)}) collective-permute-start(bf16[1024,768]{1,0:T(8,128)(2,1)S(1)} %bitcast.13), channel_id=1, source_target_pairs={{0,1},{1,0},{2,3},{3,2},{4,5},{5,4},{6,7},{7,6},{8,9},{9,8},{10,11... | collective-permute-start | bytes 4718600 | tf_op jit(solution)/shard_map/ppermute | solution.py:185
  50.7 0.0 copy-done
  50.7 2.7 %local_softmax.2 = (f32[1024,768]{1,0:T(8,128)S(1)}, f32[1,768]{1,0:T(1,128)S(1)}, f32[1,768]{1,0:T(1,128)S(1)}, f32[1024,128]{1,0:T(8,128)S(1)}) custom-call(bf16[1024,1024]{1,0:T(8,128)(2,1)S(1)} %copy-done, bf16[1024,768]{1,0:T(8,128)(2,1)S(1)} %bitcast.14), custom_call_target="tpu_custom_call" | custom-call | flops 1610612736 | bytes 6291456 | tf_op jit(solution)/shard_map/local_softmax/pallas_call | solution.py:69
  53.5 0.6 collective-permute-done.points_ref.refs_5_
  54.1 2.5 %local_softmax.3 = (f32[1024,768]{1,0:T(8,128)S(1)}, f32[1,768]{1,0:T(1,128)S(1)}, f32[1,768]{1,0:T(1,128)S(1)}) custom-call(bf16[1024,1024]{1,0:T(8,128)(2,1)S(1)} %copy-done, bf16[1024,768]{1,0:T(8,128)(2,1)S(1)} %collective-permute-done.points_ref.refs_5_, f32[1024,128]{1,0:T(8,128)S(1)} %get-tuple-element.28.norm_ref), custom_call_target="tpu_custom_call" | custom-call | flops 1610612736 | bytes 6291456 | tf_op jit(solution)/shard_map/local_softmax/pallas_call | solution.py:69
  56.6 2.0 %collective-permute-start.1 = (f32[1,1536]{1,0:T(1,128)S(1)}, f32[1,1536]{1,0:T(1,128)S(1)}, u32[]{:S(2)}, u32[]{:S(2)}) collective-permute-start(f32[1,1536]{1,0:T(1,128)S(1)} %pad_maximum_fusion.3), channel_id=1, source_target_pairs={{0,1},{1,0},{2,3},{3,2},{4,5},{5,4},{6,7},{7,6},{8,9},{9,8},{10,11... | collective-permute-start | bytes 18440 | tf_op jit(solution)/shard_map/ppermute | solution.py:185
  58.6 1.0 collective-permute-done.1
  59.6 0.1 fusion
  59.7 0.1 broadcast_in_dim.21
  59.8 17.0 %all_to_all.20 = f32[32,1,1536]{2,1,0:T(1,128)S(1)} all-to-all(f32[32,1,1536]{2,1,0:T(1,128)S(1)} %broadcast_in_dim.21), channel_id=1, replica_groups=mesh['dp'=8,'x'=4,'z'=8,'core'=2] {'x','z'}, dimensions={0} | all-to-all | bytes 393216 | tf_op jit(solution)/shard_map/all_to_all | solution.py:190
  76.8 1.1 weighted_sums.4
  78.0 5.4 %collective-permute-start.4 = (bf16[512,128]{1,0:T(8,128)(2,1)S(1)}, bf16[512,128]{1,0:T(8,128)(2,1)S(1)}, u32[]{:S(2)}, u32[]{:S(2)}) collective-permute-start(bf16[512,128]{1,0:T(8,128)(2,1)S(1)} %get-tuple-element.34), channel_id=1, source_target_pairs={{64,0},{128,64},{192,128},{256,192},{320,256},{384,320},{448,384},... | collective-permute-start | bytes 393224 | tf_op jit(solution)/shard_map/ppermute | solution.py:205
  83.4 1.9 %collective-permute-start.2 = (bf16[528,128]{1,0:T(8,128)(2,1)S(1)}, bf16[528,128]{1,0:T(8,128)(2,1)S(1)}, u32[]{:S(2)}, u32[]{:S(2)}) collective-permute-start(bf16[528,128]{1,0:T(8,128)(2,1)S(1)} %get-tuple-element.37), channel_id=1, source_target_pairs={{448,0},{0,64},{64,128},{128,192},{192,256},{256,320},{320,384},{3... | collective-permute-start | bytes 405512 | tf_op jit(solution)/shard_map/ppermute | solution.py:205
  85.3 1.0 weighted_sums.5
  86.4 0.0 collective-permute-done.4
  86.5 5.1 %collective-permute-start.5 = (bf16[1040,128]{1,0:T(8,128)(2,1)S(1)}, bf16[1040,128]{1,0:T(8,128)(2,1)S(1)}, u32[]{:S(2)}, u32[]{:S(2)}) collective-permute-start(bf16[1040,128]{1,0:T(8,128)(2,1)S(1)} %pad_maximum_fusion.1), channel_id=1, source_target_pairs={{64,0},{128,64},{192,128},{256,192},{320,256},{384,320},{448,384},... | collective-permute-start | bytes 798728 | tf_op jit(solution)/shard_map/ppermute | solution.py:205
  91.6 0.0 collective-permute-done.2
  91.7 1.9 %collective-permute-start.3 = (bf16[1040,128]{1,0:T(8,128)(2,1)S(1)}, bf16[1040,128]{1,0:T(8,128)(2,1)S(1)}, u32[]{:S(2)}, u32[]{:S(2)}) collective-permute-start(bf16[1040,128]{1,0:T(8,128)(2,1)S(1)} %pad_maximum_fusion), channel_id=1, source_target_pairs={{448,0},{0,64},{64,128},{128,192},{192,256},{256,320},{320,384},{3... | collective-permute-start | bytes 798728 | tf_op jit(solution)/shard_map/ppermute | solution.py:205
  93.6 1.0 weighted_sums.7
  94.7 1.2 %collective-permute-done.5 = bf16[1040,128]{1,0:T(8,128)(2,1)S(1)} collective-permute-done((bf16[1040,128]{1,0:T(8,128)(2,1)S(1)}, bf16[1040,128]{1,0:T(8,128)(2,1)S(1)}, u32[]{:S(2)}, u32[]{:S(2)}) %collective-permute-start.5) | collective-permute-done | bytes 266272 | tf_op jit(solution)/shard_map/ppermute | solution.py:205
  95.9 0.1 add_convert_fusion.3
  96.0 5.6 %collective-permute-start.6 = (bf16[1040,128]{1,0:T(8,128)(2,1)S(1)}, bf16[1040,128]{1,0:T(8,128)(2,1)S(1)}, u32[]{:S(2)}, u32[]{:S(2)}) collective-permute-start(bf16[1040,128]{1,0:T(8,128)(2,1)S(1)} %add_convert_fusion.3), channel_id=1, source_target_pairs={{64,0},{128,64},{192,128},{256,192},{320,256},{384,320},{448,384},... | collective-permute-start | bytes 798728 | tf_op jit(solution)/shard_map/ppermute | solution.py:205
  101.6 0.0 collective-permute-done.3
  101.6 0.1 add_convert_fusion.1
  101.7 1.9 %collective-permute-start.8 = (bf16[1040,128]{1,0:T(8,128)(2,1)S(1)}, bf16[1040,128]{1,0:T(8,128)(2,1)S(1)}, u32[]{:S(2)}, u32[]{:S(2)}) collective-permute-start(bf16[1040,128]{1,0:T(8,128)(2,1)S(1)} %add_convert_fusion.1), channel_id=1, source_target_pairs={{448,0},{0,64},{64,128},{128,192},{192,256},{256,320},{320,384},{3... | collective-permute-start | bytes 798728 | tf_op jit(solution)/shard_map/ppermute | solution.py:205
  103.6 1.5 %weighted_sums.6 = (bf16[1040,128]{1,0:T(8,128)(2,1)S(1)}, bf16[1040,128]{1,0:T(8,128)(2,1)S(1)}, bf16[1040,128]{1,0:T(8,128)(2,1)S(1)}) custom-call(s32[1]{0:T(128)} %bitcast.place_ref, f32[32,1536]{1,0:T(8,128)S(1)} %bitcast.22, f32[1024,768]{1,0:T(8,128)S(1)} %get-tuple-element.30.refs_0_, f32[1,768]{1,0:T(1,128)S(1)} %get-tuple-element.31.refs_1_, ...), custom_call_target="tpu_custom_call" | custom-call | flops 1207959552 | bytes 4718592 | tf_op jit(solution)/shard_map/weighted_sums/pallas_call | solution.py:140
  105.1 0.4 collective-permute-done.6
  105.5 0.1 add_convert_fusion.2
  105.6 5.6 %collective-permute-start.7 = (bf16[1040,128]{1,0:T(8,128)(2,1)S(1)}, bf16[1040,128]{1,0:T(8,128)(2,1)S(1)}, u32[]{:S(2)}, u32[]{:S(2)}) collective-permute-start(bf16[1040,128]{1,0:T(8,128)(2,1)S(1)} %add_convert_fusion.2), channel_id=1, source_target_pairs={{64,0},{128,64},{192,128},{256,192},{320,256},{384,320},{448,384},... | collective-permute-start | bytes 798728 | tf_op jit(solution)/shard_map/ppermute | solution.py:205
  111.2 0.0 collective-permute-done.8
  111.2 0.1 add_convert_fusion
  111.3 1.9 %collective-permute-start.9 = (bf16[1040,128]{1,0:T(8,128)(2,1)S(1)}, bf16[1040,128]{1,0:T(8,128)(2,1)S(1)}, u32[]{:S(2)}, u32[]{:S(2)}) collective-permute-start(bf16[1040,128]{1,0:T(8,128)(2,1)S(1)} %add_convert_fusion), channel_id=1, source_target_pairs={{448,0},{0,64},{64,128},{128,192},{192,256},{256,320},{320,384},{3... | collective-permute-start | bytes 798728 | tf_op jit(solution)/shard_map/ppermute | solution.py:205
  113.2 1.9 %collective-permute-done.7.down_ref = bf16[1040,128]{1,0:T(8,128)(2,1)S(1)} collective-permute-done((bf16[1040,128]{1,0:T(8,128)(2,1)S(1)}, bf16[1040,128]{1,0:T(8,128)(2,1)S(1)}, u32[]{:S(2)}, u32[]{:S(2)}) %collective-permute-start.7) | collective-permute-done | bytes 266272 | tf_op jit(solution)/shard_map/ppermute | solution.py:205
  115.1 5.7 %collective-permute-done.9.up_ref = bf16[1040,128]{1,0:T(8,128)(2,1)S(1)} collective-permute-done((bf16[1040,128]{1,0:T(8,128)(2,1)S(1)}, bf16[1040,128]{1,0:T(8,128)(2,1)S(1)}, u32[]{:S(2)}, u32[]{:S(2)}) %collective-permute-start.9) | collective-permute-done | bytes 266272 | tf_op jit(solution)/shard_map/ppermute | solution.py:205
  120.8 0.9 finish.1
  (12 shorter events, 0.2 us)
Async XLA Ops:
  23.1 27.6 %copy-start = (bf16[1024,1024]{1,0:T(8,128)(2,1)S(1)}, bf16[1024,1024]{1,0:T(8,128)(2,1)}, u32[]{:S(2)}) copy-start(bf16[1024,1024]{1,0:T(8,128)(2,1)} %cent_ref.3) | copy-start | bytes 6291460
  48.8 5.3 %collective-permute-start = (bf16[1024,768]{1,0:T(8,128)(2,1)S(1)}, bf16[1024,768]{1,0:T(8,128)(2,1)S(1)}, u32[]{:S(2)}, u32[]{:S(2)}) collective-permute-start(bf16[1024,768]{1,0:T(8,128)(2,1)S(1)} %bitcast.13), channel_id=1, source_target_pairs={{0,1},{1,0},{2,3},{3,2},{4,5},{5,4},{6,7},{7,6},{8,9},{9,8},{10,11... | collective-permute-start | bytes 4718600 | tf_op jit(solution)/shard_map/ppermute | solution.py:185
  56.6 3.1 %collective-permute-start.1 = (f32[1,1536]{1,0:T(1,128)S(1)}, f32[1,1536]{1,0:T(1,128)S(1)}, u32[]{:S(2)}, u32[]{:S(2)}) collective-permute-start(f32[1,1536]{1,0:T(1,128)S(1)} %pad_maximum_fusion.3), channel_id=1, source_target_pairs={{0,1},{1,0},{2,3},{3,2},{4,5},{5,4},{6,7},{7,6},{8,9},{9,8},{10,11... | collective-permute-start | bytes 18440 | tf_op jit(solution)/shard_map/ppermute | solution.py:185
  78.0 8.4 %collective-permute-start.4 = (bf16[512,128]{1,0:T(8,128)(2,1)S(1)}, bf16[512,128]{1,0:T(8,128)(2,1)S(1)}, u32[]{:S(2)}, u32[]{:S(2)}) collective-permute-start(bf16[512,128]{1,0:T(8,128)(2,1)S(1)} %get-tuple-element.34), channel_id=1, source_target_pairs={{64,0},{128,64},{192,128},{256,192},{320,256},{384,320},{448,384},... | collective-permute-start | bytes 393224 | tf_op jit(solution)/shard_map/ppermute | solution.py:205
  83.4 8.2 %collective-permute-start.2 = (bf16[528,128]{1,0:T(8,128)(2,1)S(1)}, bf16[528,128]{1,0:T(8,128)(2,1)S(1)}, u32[]{:S(2)}, u32[]{:S(2)}) collective-permute-start(bf16[528,128]{1,0:T(8,128)(2,1)S(1)} %get-tuple-element.37), channel_id=1, source_target_pairs={{448,0},{0,64},{64,128},{128,192},{192,256},{256,320},{320,384},{3... | collective-permute-start | bytes 405512 | tf_op jit(solution)/shard_map/ppermute | solution.py:205
  86.5 9.5 %collective-permute-start.5 = (bf16[1040,128]{1,0:T(8,128)(2,1)S(1)}, bf16[1040,128]{1,0:T(8,128)(2,1)S(1)}, u32[]{:S(2)}, u32[]{:S(2)}) collective-permute-start(bf16[1040,128]{1,0:T(8,128)(2,1)S(1)} %pad_maximum_fusion.1), channel_id=1, source_target_pairs={{64,0},{128,64},{192,128},{256,192},{320,256},{384,320},{448,384},... | collective-permute-start | bytes 798728 | tf_op jit(solution)/shard_map/ppermute | solution.py:205
  91.7 9.9 %collective-permute-start.3 = (bf16[1040,128]{1,0:T(8,128)(2,1)S(1)}, bf16[1040,128]{1,0:T(8,128)(2,1)S(1)}, u32[]{:S(2)}, u32[]{:S(2)}) collective-permute-start(bf16[1040,128]{1,0:T(8,128)(2,1)S(1)} %pad_maximum_fusion), channel_id=1, source_target_pairs={{448,0},{0,64},{64,128},{128,192},{192,256},{256,320},{320,384},{3... | collective-permute-start | bytes 798728 | tf_op jit(solution)/shard_map/ppermute | solution.py:205
  96.0 9.5 %collective-permute-start.6 = (bf16[1040,128]{1,0:T(8,128)(2,1)S(1)}, bf16[1040,128]{1,0:T(8,128)(2,1)S(1)}, u32[]{:S(2)}, u32[]{:S(2)}) collective-permute-start(bf16[1040,128]{1,0:T(8,128)(2,1)S(1)} %add_convert_fusion.3), channel_id=1, source_target_pairs={{64,0},{128,64},{192,128},{256,192},{320,256},{384,320},{448,384},... | collective-permute-start | bytes 798728 | tf_op jit(solution)/shard_map/ppermute | solution.py:205
  101.7 9.5 %collective-permute-start.8 = (bf16[1040,128]{1,0:T(8,128)(2,1)S(1)}, bf16[1040,128]{1,0:T(8,128)(2,1)S(1)}, u32[]{:S(2)}, u32[]{:S(2)}) collective-permute-start(bf16[1040,128]{1,0:T(8,128)(2,1)S(1)} %add_convert_fusion.1), channel_id=1, source_target_pairs={{448,0},{0,64},{64,128},{128,192},{192,256},{256,320},{320,384},{3... | collective-permute-start | bytes 798728 | tf_op jit(solution)/shard_map/ppermute | solution.py:205
  105.6 9.5 %collective-permute-start.7 = (bf16[1040,128]{1,0:T(8,128)(2,1)S(1)}, bf16[1040,128]{1,0:T(8,128)(2,1)S(1)}, u32[]{:S(2)}, u32[]{:S(2)}) collective-permute-start(bf16[1040,128]{1,0:T(8,128)(2,1)S(1)} %add_convert_fusion.2), channel_id=1, source_target_pairs={{64,0},{128,64},{192,128},{256,192},{320,256},{384,320},{448,384},... | collective-permute-start | bytes 798728 | tf_op jit(solution)/shard_map/ppermute | solution.py:205
  111.3 9.5 %collective-permute-start.9 = (bf16[1040,128]{1,0:T(8,128)(2,1)S(1)}, bf16[1040,128]{1,0:T(8,128)(2,1)S(1)}, u32[]{:S(2)}, u32[]{:S(2)}) collective-permute-start(bf16[1040,128]{1,0:T(8,128)(2,1)S(1)} %add_convert_fusion), channel_id=1, source_target_pairs={{448,0},{0,64},{64,128},{128,192},{192,256},{256,320},{320,384},{3... | collective-permute-start | bytes 798728 | tf_op jit(solution)/shard_map/ppermute | solution.py:205

commit v5 on v4

--- a/solution.py
+++ b/solution.py
@@ -12,6 +12,7 @@
 lanes = 128
 tile = 256
 tall = 512
+short = 256
 count_rows = 16
 vmem = pl.BlockSpec(memory_space=pltpu.VMEM)
 smem = pl.BlockSpec(memory_space=pltpu.SMEM)
@@ -33,7 +34,7 @@
 
 def logits_kernel(cent_ref, points_ref, norm_ref, raised_ref, peak_ref, lse_ref):
     n_cent, n_tok = raised_ref.shape
-    row_blocks = [pl.ds(r, tall) for r in range(0, n_cent, tall)]
+    row_blocks = [pl.ds(r, short) for r in range(0, n_cent, short)]
     token_blocks = [pl.ds(t, tile) for t in range(0, n_tok, tile)]
     peaks = []
     for step in range(len(token_blocks) + 1):

time: 122 us -> 122 us (level)
  no operation moved by 1% of the time
where the time goes in v5:
time: 122 us
  blocking collectives  64.3 us (53%)
  starting transfers between devices  33.3 us (27%)
  waiting for transfers between devices  11 us (9%)
  Pallas kernels  10.7 us (9%)
    all_to_all x2, blocking collectives, spread(): lax.all_to_all(jnp.broadcast_to(value[None], (n,) + value.shape), axis, 0...  42.6 us
    ppermute x8, starting transfers between devices, dp_shift(): return lax.ppermute(value, 'dp', [((i + d) % n, i) for i in range(n)])  29.4 us
    all_to_all x1, blocking collectives, gather_half(): lax.all_to_all(blocks, ('z', 'core'), 0, 0).reshape(-1, n_tok // n_core)  21.7 us
    ppermute x8, waiting for transfers between devices, dp_shift(): return lax.ppermute(value, 'dp', [((i + d) % n, i) for i in range(n)])  9.28 us
    pallas_call x2, Pallas kernels, local_softmax(): pl.pallas_call(norms_kernel if norms is None else logits_kernel, out_shap...  5.1 us
    pallas_call x4, Pallas kernels, weighted_sums(): pl.pallas_call(functools.partial(sums_kernel, order, n_blocks), out_shape...  4.71 us
    ppermute x2, starting transfers between devices, core_swap(): return lax.ppermute(value, 'core', [(0, 1), (1, 0)])  3.95 us
  transfers between devices with their start and end apart: 10, of which 6 were waited for; matrix products, arithmetic and copies ran while one was open for 0% of the time, Pallas kernels for 5%

profile of v5, /device:TPU:64, one launch (start us, length us, event | category | flops | bytes accessed | tf_op | source)
XLA Modules:
  0.0 121.7 jit_solution(10598076322136740092)
XLA Ops:
  0.6 0.8 slice_bitcast_fusion.1
  1.4 21.7 %all_to_all.18 = bf16[16,16,768]{2,1,0:T(8,128)(2,1)S(1)} all-to-all(bf16[16,16,768]{2,1,0:T(8,128)(2,1)S(1)} %bitcast.23), channel_id=1, replica_groups=mesh['dp'=8,'x'=4,'z'=8,'core'=2] {'z','core'}, dimensions={0} | all-to-all | bytes 786432 | tf_op jit(solution)/shard_map/all_to_all | solution.py:200
  23.1 0.0 copy-start
  23.1 0.1 broadcast_in_dim.20
  23.2 25.6 %all_to_all.19 = bf16[4,256,768]{2,1,0:T(8,128)(2,1)S(1)} all-to-all(bf16[4,256,768]{2,1,0:T(8,128)(2,1)S(1)} %broadcast_in_dim.20), channel_id=1, replica_groups=mesh['dp'=8,'x'=4,'z'=8,'core'=2] {'x'}, dimensions={0} | all-to-all | bytes 3145728 | tf_op jit(solution)/shard_map/all_to_all | solution.py:191
  48.8 1.9 %collective-permute-start = (bf16[1024,768]{1,0:T(8,128)(2,1)S(1)}, bf16[1024,768]{1,0:T(8,128)(2,1)S(1)}, u32[]{:S(2)}, u32[]{:S(2)}) collective-permute-start(bf16[1024,768]{1,0:T(8,128)(2,1)S(1)} %bitcast.13), channel_id=1, source_target_pairs={{0,1},{1,0},{2,3},{3,2},{4,5},{5,4},{6,7},{7,6},{8,9},{9,8},{10,11... | collective-permute-start | bytes 4718600 | tf_op jit(solution)/shard_map/ppermute | solution.py:186
  50.7 0.0 copy-done
  50.7 2.7 %local_softmax.2 = (f32[1024,768]{1,0:T(8,128)S(1)}, f32[1,768]{1,0:T(1,128)S(1)}, f32[1,768]{1,0:T(1,128)S(1)}, f32[1024,128]{1,0:T(8,128)S(1)}) custom-call(bf16[1024,1024]{1,0:T(8,128)(2,1)S(1)} %copy-done, bf16[1024,768]{1,0:T(8,128)(2,1)S(1)} %bitcast.14), custom_call_target="tpu_custom_call" | custom-call | flops 1610612736 | bytes 6291456 | tf_op jit(solution)/shard_map/local_softmax/pallas_call | solution.py:70
  53.4 0.7 collective-permute-done.points_ref.refs_5_
  54.1 2.4 %local_softmax.3 = (f32[1024,768]{1,0:T(8,128)S(1)}, f32[1,768]{1,0:T(1,128)S(1)}, f32[1,768]{1,0:T(1,128)S(1)}) custom-call(bf16[1024,1024]{1,0:T(8,128)(2,1)S(1)} %copy-done, bf16[1024,768]{1,0:T(8,128)(2,1)S(1)} %collective-permute-done.points_ref.refs_5_, f32[1024,128]{1,0:T(8,128)S(1)} %get-tuple-element.28.norm_ref), custom_call_target="tpu_custom_call" | custom-call | flops 1610612736 | bytes 6291456 | tf_op jit(solution)/shard_map/local_softmax/pallas_call | solution.py:70
  56.6 2.0 %collective-permute-start.1 = (f32[1,1536]{1,0:T(1,128)S(1)}, f32[1,1536]{1,0:T(1,128)S(1)}, u32[]{:S(2)}, u32[]{:S(2)}) collective-permute-start(f32[1,1536]{1,0:T(1,128)S(1)} %pad_maximum_fusion.3), channel_id=1, source_target_pairs={{0,1},{1,0},{2,3},{3,2},{4,5},{5,4},{6,7},{7,6},{8,9},{9,8},{10,11... | collective-permute-start | bytes 18440 | tf_op jit(solution)/shard_map/ppermute | solution.py:186
  58.6 1.0 collective-permute-done.1
  59.6 0.1 fusion
  59.7 0.1 broadcast_in_dim.21
  59.8 17.0 %all_to_all.20 = f32[32,1,1536]{2,1,0:T(1,128)S(1)} all-to-all(f32[32,1,1536]{2,1,0:T(1,128)S(1)} %broadcast_in_dim.21), channel_id=1, replica_groups=mesh['dp'=8,'x'=4,'z'=8,'core'=2] {'x','z'}, dimensions={0} | all-to-all | bytes 393216 | tf_op jit(solution)/shard_map/all_to_all | solution.py:191
  76.8 1.1 weighted_sums.4
  78.0 5.4 %collective-permute-start.4 = (bf16[512,128]{1,0:T(8,128)(2,1)S(1)}, bf16[512,128]{1,0:T(8,128)(2,1)S(1)}, u32[]{:S(2)}, u32[]{:S(2)}) collective-permute-start(bf16[512,128]{1,0:T(8,128)(2,1)S(1)} %get-tuple-element.34), channel_id=1, source_target_pairs={{64,0},{128,64},{192,128},{256,192},{320,256},{384,320},{448,384},... | collective-permute-start | bytes 393224 | tf_op jit(solution)/shard_map/ppermute | solution.py:206
  83.3 1.9 %collective-permute-start.2 = (bf16[528,128]{1,0:T(8,128)(2,1)S(1)}, bf16[528,128]{1,0:T(8,128)(2,1)S(1)}, u32[]{:S(2)}, u32[]{:S(2)}) collective-permute-start(bf16[528,128]{1,0:T(8,128)(2,1)S(1)} %get-tuple-element.37), channel_id=1, source_target_pairs={{448,0},{0,64},{64,128},{128,192},{192,256},{256,320},{320,384},{3... | collective-permute-start | bytes 405512 | tf_op jit(solution)/shard_map/ppermute | solution.py:206
  85.3 1.0 weighted_sums.5
  86.4 0.0 collective-permute-done.4
  86.4 5.1 %collective-permute-start.5 = (bf16[1040,128]{1,0:T(8,128)(2,1)S(1)}, bf16[1040,128]{1,0:T(8,128)(2,1)S(1)}, u32[]{:S(2)}, u32[]{:S(2)}) collective-permute-start(bf16[1040,128]{1,0:T(8,128)(2,1)S(1)} %pad_maximum_fusion.1), channel_id=1, source_target_pairs={{64,0},{128,64},{192,128},{256,192},{320,256},{384,320},{448,384},... | collective-permute-start | bytes 798728 | tf_op jit(solution)/shard_map/ppermute | solution.py:206
  91.6 0.0 collective-permute-done.2
  91.7 1.9 %collective-permute-start.3 = (bf16[1040,128]{1,0:T(8,128)(2,1)S(1)}, bf16[1040,128]{1,0:T(8,128)(2,1)S(1)}, u32[]{:S(2)}, u32[]{:S(2)}) collective-permute-start(bf16[1040,128]{1,0:T(8,128)(2,1)S(1)} %pad_maximum_fusion), channel_id=1, source_target_pairs={{448,0},{0,64},{64,128},{128,192},{192,256},{256,320},{320,384},{3... | collective-permute-start | bytes 798728 | tf_op jit(solution)/shard_map/ppermute | solution.py:206
  93.6 1.0 weighted_sums.7
  94.6 1.2 %collective-permute-done.5 = bf16[1040,128]{1,0:T(8,128)(2,1)S(1)} collective-permute-done((bf16[1040,128]{1,0:T(8,128)(2,1)S(1)}, bf16[1040,128]{1,0:T(8,128)(2,1)S(1)}, u32[]{:S(2)}, u32[]{:S(2)}) %collective-permute-start.5) | collective-permute-done | bytes 266272 | tf_op jit(solution)/shard_map/ppermute | solution.py:206
  95.9 0.1 add_convert_fusion.3
  96.0 5.6 %collective-permute-start.6 = (bf16[1040,128]{1,0:T(8,128)(2,1)S(1)}, bf16[1040,128]{1,0:T(8,128)(2,1)S(1)}, u32[]{:S(2)}, u32[]{:S(2)}) collective-permute-start(bf16[1040,128]{1,0:T(8,128)(2,1)S(1)} %add_convert_fusion.3), channel_id=1, source_target_pairs={{64,0},{128,64},{192,128},{256,192},{320,256},{384,320},{448,384},... | collective-permute-start | bytes 798728 | tf_op jit(solution)/shard_map/ppermute | solution.py:206
  101.6 0.0 collective-permute-done.3
  101.6 0.1 add_convert_fusion.1
  101.7 1.9 %collective-permute-start.8 = (bf16[1040,128]{1,0:T(8,128)(2,1)S(1)}, bf16[1040,128]{1,0:T(8,128)(2,1)S(1)}, u32[]{:S(2)}, u32[]{:S(2)}) collective-permute-start(bf16[1040,128]{1,0:T(8,128)(2,1)S(1)} %add_convert_fusion.1), channel_id=1, source_target_pairs={{448,0},{0,64},{64,128},{128,192},{192,256},{256,320},{320,384},{3... | collective-permute-start | bytes 798728 | tf_op jit(solution)/shard_map/ppermute | solution.py:206
  103.6 1.5 %weighted_sums.6 = (bf16[1040,128]{1,0:T(8,128)(2,1)S(1)}, bf16[1040,128]{1,0:T(8,128)(2,1)S(1)}, bf16[1040,128]{1,0:T(8,128)(2,1)S(1)}) custom-call(s32[1]{0:T(128)} %bitcast.place_ref, f32[32,1536]{1,0:T(8,128)S(1)} %bitcast.22, f32[1024,768]{1,0:T(8,128)S(1)} %get-tuple-element.30.refs_0_, f32[1,768]{1,0:T(1,128)S(1)} %get-tuple-element.31.refs_1_, ...), custom_call_target="tpu_custom_call" | custom-call | flops 1207959552 | bytes 4718592 | tf_op jit(solution)/shard_map/weighted_sums/pallas_call | solution.py:141
  105.1 0.4 collective-permute-done.6
  105.5 0.1 add_convert_fusion.2
  105.6 5.6 %collective-permute-start.7 = (bf16[1040,128]{1,0:T(8,128)(2,1)S(1)}, bf16[1040,128]{1,0:T(8,128)(2,1)S(1)}, u32[]{:S(2)}, u32[]{:S(2)}) collective-permute-start(bf16[1040,128]{1,0:T(8,128)(2,1)S(1)} %add_convert_fusion.2), channel_id=1, source_target_pairs={{64,0},{128,64},{192,128},{256,192},{320,256},{384,320},{448,384},... | collective-permute-start | bytes 798728 | tf_op jit(solution)/shard_map/ppermute | solution.py:206
  111.2 0.0 collective-permute-done.8
  111.2 0.1 add_convert_fusion
  111.3 1.9 %collective-permute-start.9 = (bf16[1040,128]{1,0:T(8,128)(2,1)S(1)}, bf16[1040,128]{1,0:T(8,128)(2,1)S(1)}, u32[]{:S(2)}, u32[]{:S(2)}) collective-permute-start(bf16[1040,128]{1,0:T(8,128)(2,1)S(1)} %add_convert_fusion), channel_id=1, source_target_pairs={{448,0},{0,64},{64,128},{128,192},{192,256},{256,320},{320,384},{3... | collective-permute-start | bytes 798728 | tf_op jit(solution)/shard_map/ppermute | solution.py:206
  113.2 1.9 %collective-permute-done.7.down_ref = bf16[1040,128]{1,0:T(8,128)(2,1)S(1)} collective-permute-done((bf16[1040,128]{1,0:T(8,128)(2,1)S(1)}, bf16[1040,128]{1,0:T(8,128)(2,1)S(1)}, u32[]{:S(2)}, u32[]{:S(2)}) %collective-permute-start.7) | collective-permute-done | bytes 266272 | tf_op jit(solution)/shard_map/ppermute | solution.py:206
  115.1 5.7 %collective-permute-done.9.up_ref = bf16[1040,128]{1,0:T(8,128)(2,1)S(1)} collective-permute-done((bf16[1040,128]{1,0:T(8,128)(2,1)S(1)}, bf16[1040,128]{1,0:T(8,128)(2,1)S(1)}, u32[]{:S(2)}, u32[]{:S(2)}) %collective-permute-start.9) | collective-permute-done | bytes 266272 | tf_op jit(solution)/shard_map/ppermute | solution.py:206
  120.8 0.9 finish.1
  (12 shorter events, 0.2 us)
Async XLA Ops:
  23.1 27.6 %copy-start = (bf16[1024,1024]{1,0:T(8,128)(2,1)S(1)}, bf16[1024,1024]{1,0:T(8,128)(2,1)}, u32[]{:S(2)}) copy-start(bf16[1024,1024]{1,0:T(8,128)(2,1)} %cent_ref.3) | copy-start | bytes 6291460
  48.8 5.3 %collective-permute-start = (bf16[1024,768]{1,0:T(8,128)(2,1)S(1)}, bf16[1024,768]{1,0:T(8,128)(2,1)S(1)}, u32[]{:S(2)}, u32[]{:S(2)}) collective-permute-start(bf16[1024,768]{1,0:T(8,128)(2,1)S(1)} %bitcast.13), channel_id=1, source_target_pairs={{0,1},{1,0},{2,3},{3,2},{4,5},{5,4},{6,7},{7,6},{8,9},{9,8},{10,11... | collective-permute-start | bytes 4718600 | tf_op jit(solution)/shard_map/ppermute | solution.py:186
  56.6 3.1 %collective-permute-start.1 = (f32[1,1536]{1,0:T(1,128)S(1)}, f32[1,1536]{1,0:T(1,128)S(1)}, u32[]{:S(2)}, u32[]{:S(2)}) collective-permute-start(f32[1,1536]{1,0:T(1,128)S(1)} %pad_maximum_fusion.3), channel_id=1, source_target_pairs={{0,1},{1,0},{2,3},{3,2},{4,5},{5,4},{6,7},{7,6},{8,9},{9,8},{10,11... | collective-permute-start | bytes 18440 | tf_op jit(solution)/shard_map/ppermute | solution.py:186
  78.0 8.4 %collective-permute-start.4 = (bf16[512,128]{1,0:T(8,128)(2,1)S(1)}, bf16[512,128]{1,0:T(8,128)(2,1)S(1)}, u32[]{:S(2)}, u32[]{:S(2)}) collective-permute-start(bf16[512,128]{1,0:T(8,128)(2,1)S(1)} %get-tuple-element.34), channel_id=1, source_target_pairs={{64,0},{128,64},{192,128},{256,192},{320,256},{384,320},{448,384},... | collective-permute-start | bytes 393224 | tf_op jit(solution)/shard_map/ppermute | solution.py:206
  83.3 8.2 %collective-permute-start.2 = (bf16[528,128]{1,0:T(8,128)(2,1)S(1)}, bf16[528,128]{1,0:T(8,128)(2,1)S(1)}, u32[]{:S(2)}, u32[]{:S(2)}) collective-permute-start(bf16[528,128]{1,0:T(8,128)(2,1)S(1)} %get-tuple-element.37), channel_id=1, source_target_pairs={{448,0},{0,64},{64,128},{128,192},{192,256},{256,320},{320,384},{3... | collective-permute-start | bytes 405512 | tf_op jit(solution)/shard_map/ppermute | solution.py:206
  86.4 9.5 %collective-permute-start.5 = (bf16[1040,128]{1,0:T(8,128)(2,1)S(1)}, bf16[1040,128]{1,0:T(8,128)(2,1)S(1)}, u32[]{:S(2)}, u32[]{:S(2)}) collective-permute-start(bf16[1040,128]{1,0:T(8,128)(2,1)S(1)} %pad_maximum_fusion.1), channel_id=1, source_target_pairs={{64,0},{128,64},{192,128},{256,192},{320,256},{384,320},{448,384},... | collective-permute-start | bytes 798728 | tf_op jit(solution)/shard_map/ppermute | solution.py:206
  91.7 9.9 %collective-permute-start.3 = (bf16[1040,128]{1,0:T(8,128)(2,1)S(1)}, bf16[1040,128]{1,0:T(8,128)(2,1)S(1)}, u32[]{:S(2)}, u32[]{:S(2)}) collective-permute-start(bf16[1040,128]{1,0:T(8,128)(2,1)S(1)} %pad_maximum_fusion), channel_id=1, source_target_pairs={{448,0},{0,64},{64,128},{128,192},{192,256},{256,320},{320,384},{3... | collective-permute-start | bytes 798728 | tf_op jit(solution)/shard_map/ppermute | solution.py:206
  96.0 9.5 %collective-permute-start.6 = (bf16[1040,128]{1,0:T(8,128)(2,1)S(1)}, bf16[1040,128]{1,0:T(8,128)(2,1)S(1)}, u32[]{:S(2)}, u32[]{:S(2)}) collective-permute-start(bf16[1040,128]{1,0:T(8,128)(2,1)S(1)} %add_convert_fusion.3), channel_id=1, source_target_pairs={{64,0},{128,64},{192,128},{256,192},{320,256},{384,320},{448,384},... | collective-permute-start | bytes 798728 | tf_op jit(solution)/shard_map/ppermute | solution.py:206
  101.7 9.5 %collective-permute-start.8 = (bf16[1040,128]{1,0:T(8,128)(2,1)S(1)}, bf16[1040,128]{1,0:T(8,128)(2,1)S(1)}, u32[]{:S(2)}, u32[]{:S(2)}) collective-permute-start(bf16[1040,128]{1,0:T(8,128)(2,1)S(1)} %add_convert_fusion.1), channel_id=1, source_target_pairs={{448,0},{0,64},{64,128},{128,192},{192,256},{256,320},{320,384},{3... | collective-permute-start | bytes 798728 | tf_op jit(solution)/shard_map/ppermute | solution.py:206
  105.6 9.5 %collective-permute-start.7 = (bf16[1040,128]{1,0:T(8,128)(2,1)S(1)}, bf16[1040,128]{1,0:T(8,128)(2,1)S(1)}, u32[]{:S(2)}, u32[]{:S(2)}) collective-permute-start(bf16[1040,128]{1,0:T(8,128)(2,1)S(1)} %add_convert_fusion.2), channel_id=1, source_target_pairs={{64,0},{128,64},{192,128},{256,192},{320,256},{384,320},{448,384},... | collective-permute-start | bytes 798728 | tf_op jit(solution)/shard_map/ppermute | solution.py:206
  111.3 9.5 %collective-permute-start.9 = (bf16[1040,128]{1,0:T(8,128)(2,1)S(1)}, bf16[1040,128]{1,0:T(8,128)(2,1)S(1)}, u32[]{:S(2)}, u32[]{:S(2)}) collective-permute-start(bf16[1040,128]{1,0:T(8,128)(2,1)S(1)} %add_convert_fusion), channel_id=1, source_target_pairs={{448,0},{0,64},{64,128},{128,192},{192,256},{256,320},{320,384},{3... | collective-permute-start | bytes 798728 | tf_op jit(solution)/shard_map/ppermute | solution.py:206

commit v6 on v4

--- a/solution.py
+++ b/solution.py
@@ -81,22 +81,15 @@
     return results if norms is None else (*results, norms)
 
 
-def sums_kernel(order, n_blocks, place_ref, lse_ref, *refs):
+def sums_kernel(order, n_blocks, span, place_ref, lse_ref, *refs):
     halves, outs, resp_ref = (refs[0:3], refs[3:6]), refs[6:-1], refs[-1]
     depth = halves[0][2].shape[0]
     share = refs[0].shape[0] // n_blocks
     n_tok = refs[0].shape[1]
-    far = len(outs) - len(order)
-    cut = outs[0].shape[0]
+    top_row = span[0] // lanes * share
 
     def put(i, start, value):
-        value = value.astype(jnp.bfloat16)
-        if i > 0 or not far:
-            outs[i + far][pl.ds(start, value.shape[0]), :] = value
-        elif start < cut:
-            outs[0][pl.ds(start, value.shape[0]), :] = value
-        else:
-            outs[1][pl.ds(start - cut, value.shape[0]), :] = value
+        outs[i][pl.ds(start - top_row, value.shape[0]), :] = value.astype(jnp.bfloat16)
 
     parts = lse_ref[...]
     top = jnp.max(parts, axis=0, keepdims=True)
@@ -112,10 +105,11 @@
             resp = (half[0][rows, :] * scales[h]).astype(jnp.bfloat16)
             resp_ref[pl.ds(i * share, share), pl.ds(h * n_tok, n_tok)] = resp
             count += jnp.sum(resp.astype(jnp.float32), axis=1, keepdims=True)
-        put(i, depth // lanes * share, jnp.transpose(jnp.broadcast_to(count, (share, lanes)))[:count_rows])
+        if span[1] == depth:
+            put(i, depth // lanes * share, jnp.transpose(jnp.broadcast_to(count, (share, lanes)))[:count_rows])
     for i in range(0, len(order), tall // share):
         rows = min(tall, (len(order) - i) * share)
-        for c in range(0, depth, tile):
+        for c in range(*span, tile):
             total = sum(
                 lax.dot_general(
                     resp_ref[pl.ds(i * share, rows), pl.ds(h * n_tok, n_tok)],
@@ -130,18 +124,18 @@
                     put(i + k, (c + p) // lanes * share, total[k * share:(k + 1) * share, p:p + lanes])
 
 
-def weighted_sums(order, n_blocks, far, place, lse, halves):
+def weighted_sums(order, n_blocks, place, lse, halves, span=None):
     n_cent, n_tok = halves[0][0].shape
     depth = halves[0][2].shape[0]
     n = len(order)
     share = n_cent // n_blocks
-    height, cut = depth // lanes * share + count_rows, depth // lanes // 2 * share
-    heights = ((cut, height - cut) if far else (height,)) + (height,) * (n - 1)
+    span = span or (0, depth)
+    height = (span[1] - span[0]) // lanes * share + (count_rows if span[1] == depth else 0)
     return pl.pallas_call(
-        functools.partial(sums_kernel, order, n_blocks),
-        out_shape=tuple(jax.ShapeDtypeStruct((h, lanes), jnp.bfloat16) for h in heights),
+        functools.partial(sums_kernel, order, n_blocks, span),
+        out_shape=(jax.ShapeDtypeStruct((height, lanes), jnp.bfloat16),) * n,
         in_specs=[smem] + [vmem] * 7,
-        out_specs=(vmem,) * len(heights),
+        out_specs=(vmem,) * n,
         scratch_shapes=[pltpu.VMEM((n * share, 2 * n_tok), jnp.bfloat16)],
         compiler_params=limit(20),
         cost_estimate=pl.CostEstimate(
@@ -220,7 +214,7 @@
 def ring_sum(far, make_near):
     down, up = dp_shift(far[0], 1), dp_shift(far[1], -1)
     starts = 0, far[0].shape[0]
-    near = make_near(far[0])
+    near = make_near(far[1])
     while len(near) > 1:
         rest = make_near(up) if len(near) == 2 else near[2:]
         down = dp_shift(add(near[0], down, starts[0]), 1)
@@ -244,12 +238,16 @@
     lse = spread(jnp.logaddexp(here, there)[0], ("x", "z"))
     halves = ((raised_0, peak_0, mine), (raised_1, peak_1, other))
     order = ring_order(n_dp)
-    far = weighted_sums(order[:1], n_dp, True, place, lse, halves)
+    depth = centroids.shape[1]
+    far = [
+        weighted_sums(order[:1], n_dp, place, lse, halves, span)[0]
+        for span in ((0, depth // 2), (depth // 2, depth))
+    ]
     rounds = [order[i:i + 2] for i in range(1, n_dp - 3, 2)] + [order[-3:]]
 
     def make_near(after):
         late, _ = lax.optimization_barrier((lse, after))
-        return weighted_sums(rounds.pop(0), n_dp, False, place, late, halves)
+        return weighted_sums(rounds.pop(0), n_dp, place, late, halves)
 
     own, down, up = ring_sum(far, make_near)
     factor = centroids.shape[0] * n_cent / (points.shape[0] * n_dp)

time: 122 us -> 122 us (level)
    pallas_call x4 -> x5, Pallas kernels: 4.71 us -> 4.89 us  [weighted_sums(): pl.pallas_call(functools.partial(sums_kernel, order, n_blocks, span), out...]
  transfers between devices with their start and end apart: 10 -> 10, of which waited for: 6 -> 6; matrix products, arithmetic and copies ran while one was open for 0% -> 0% of each run, Pallas kernels for 5% -> 6%
where the time goes in v6:
time: 122 us
  blocking collectives  64.3 us (53%)
  starting transfers between devices  33.3 us (27%)
  Pallas kernels  11 us (9%)
  waiting for transfers between devices  10.9 us (9%)
    all_to_all x2, blocking collectives, spread(): lax.all_to_all(jnp.broadcast_to(value[None], (n,) + value.shape), axis, 0...  42.6 us
    ppermute x8, starting transfers between devices, dp_shift(): return lax.ppermute(value, 'dp', [((i + d) % n, i) for i in range(n)])  29.4 us
    all_to_all x1, blocking collectives, gather_half(): lax.all_to_all(blocks, ('z', 'core'), 0, 0).reshape(-1, n_tok // n_core)  21.7 us
    ppermute x8, waiting for transfers between devices, dp_shift(): return lax.ppermute(value, 'dp', [((i + d) % n, i) for i in range(n)])  9.27 us
    pallas_call x2, Pallas kernels, local_softmax(): pl.pallas_call(norms_kernel if norms is None else logits_kernel, out_shap...  5.17 us
    pallas_call x5, Pallas kernels, weighted_sums(): pl.pallas_call(functools.partial(sums_kernel, order, n_blocks, span), out...  4.89 us
    ppermute x2, starting transfers between devices, core_swap(): return lax.ppermute(value, 'core', [(0, 1), (1, 0)])  3.95 us
  transfers between devices with their start and end apart: 10, of which 6 were waited for; matrix products, arithmetic and copies ran while one was open for 0% of the time, Pallas kernels for 6%

profile of v6, /device:TPU:64, one launch (start us, length us, event | category | flops | bytes accessed | tf_op | source)
XLA Modules:
  0.0 121.9 jit_solution(6839487684990773772)
XLA Ops:
  0.6 0.8 slice_bitcast_fusion.1
  1.4 21.7 %all_to_all.18 = bf16[16,16,768]{2,1,0:T(8,128)(2,1)S(1)} all-to-all(bf16[16,16,768]{2,1,0:T(8,128)(2,1)S(1)} %bitcast.25), channel_id=1, replica_groups=mesh['dp'=8,'x'=4,'z'=8,'core'=2] {'z','core'}, dimensions={0} | all-to-all | bytes 786432 | tf_op jit(solution)/shard_map/all_to_all | solution.py:193
  23.1 0.0 copy-start
  23.1 0.1 broadcast_in_dim.20
  23.2 25.6 %all_to_all.19 = bf16[4,256,768]{2,1,0:T(8,128)(2,1)S(1)} all-to-all(bf16[4,256,768]{2,1,0:T(8,128)(2,1)S(1)} %broadcast_in_dim.20), channel_id=1, replica_groups=mesh['dp'=8,'x'=4,'z'=8,'core'=2] {'x'}, dimensions={0} | all-to-all | bytes 3145728 | tf_op jit(solution)/shard_map/all_to_all | solution.py:184
  48.8 1.9 %collective-permute-start = (bf16[1024,768]{1,0:T(8,128)(2,1)S(1)}, bf16[1024,768]{1,0:T(8,128)(2,1)S(1)}, u32[]{:S(2)}, u32[]{:S(2)}) collective-permute-start(bf16[1024,768]{1,0:T(8,128)(2,1)S(1)} %bitcast.13), channel_id=1, source_target_pairs={{0,1},{1,0},{2,3},{3,2},{4,5},{5,4},{6,7},{7,6},{8,9},{9,8},{10,11... | collective-permute-start | bytes 4718600 | tf_op jit(solution)/shard_map/ppermute | solution.py:179
  50.7 0.0 copy-done
  50.7 2.7 %local_softmax.2 = (f32[1024,768]{1,0:T(8,128)S(1)}, f32[1,768]{1,0:T(1,128)S(1)}, f32[1,768]{1,0:T(1,128)S(1)}, f32[1024,128]{1,0:T(8,128)S(1)}) custom-call(bf16[1024,1024]{1,0:T(8,128)(2,1)S(1)} %copy-done, bf16[1024,768]{1,0:T(8,128)(2,1)S(1)} %bitcast.14), custom_call_target="tpu_custom_call" | custom-call | flops 1610612736 | bytes 6291456 | tf_op jit(solution)/shard_map/local_softmax/pallas_call | solution.py:69
  53.5 0.6 collective-permute-done.points_ref.refs_5_
  54.1 2.5 %local_softmax.3 = (f32[1024,768]{1,0:T(8,128)S(1)}, f32[1,768]{1,0:T(1,128)S(1)}, f32[1,768]{1,0:T(1,128)S(1)}) custom-call(bf16[1024,1024]{1,0:T(8,128)(2,1)S(1)} %copy-done, bf16[1024,768]{1,0:T(8,128)(2,1)S(1)} %collective-permute-done.points_ref.refs_5_, f32[1024,128]{1,0:T(8,128)S(1)} %get-tuple-element.26.norm_ref), custom_call_target="tpu_custom_call" | custom-call | flops 1610612736 | bytes 6291456 | tf_op jit(solution)/shard_map/local_softmax/pallas_call | solution.py:69
  56.6 2.0 %collective-permute-start.1 = (f32[1,1536]{1,0:T(1,128)S(1)}, f32[1,1536]{1,0:T(1,128)S(1)}, u32[]{:S(2)}, u32[]{:S(2)}) collective-permute-start(f32[1,1536]{1,0:T(1,128)S(1)} %pad_maximum_fusion.3), channel_id=1, source_target_pairs={{0,1},{1,0},{2,3},{3,2},{4,5},{5,4},{6,7},{7,6},{8,9},{9,8},{10,11... | collective-permute-start | bytes 18440 | tf_op jit(solution)/shard_map/ppermute | solution.py:179
  58.6 1.0 collective-permute-done.1
  59.6 0.1 fusion
  59.7 0.1 broadcast_in_dim.21
  59.8 17.0 %all_to_all.20 = f32[32,1,1536]{2,1,0:T(1,128)S(1)} all-to-all(f32[32,1,1536]{2,1,0:T(1,128)S(1)} %broadcast_in_dim.21), channel_id=1, replica_groups=mesh['dp'=8,'x'=4,'z'=8,'core'=2] {'x','z'}, dimensions={0} | all-to-all | bytes 393216 | tf_op jit(solution)/shard_map/all_to_all | solution.py:184
  76.8 0.7 weighted_sums.9
  77.5 5.4 %collective-permute-start.4 = (bf16[512,128]{1,0:T(8,128)(2,1)S(1)}, bf16[512,128]{1,0:T(8,128)(2,1)S(1)}, u32[]{:S(2)}, u32[]{:S(2)}) collective-permute-start(bf16[512,128]{1,0:T(8,128)(2,1)S(1)} %weighted_sums.9), channel_id=1, source_target_pairs={{64,0},{128,64},{192,128},{256,192},{320,256},{384,320},{448,384},... | collective-permute-start | bytes 393224 | tf_op jit(solution)/shard_map/ppermute | solution.py:199
  82.9 0.7 weighted_sums.5
  83.6 1.9 %collective-permute-start.2 = (bf16[528,128]{1,0:T(8,128)(2,1)S(1)}, bf16[528,128]{1,0:T(8,128)(2,1)S(1)}, u32[]{:S(2)}, u32[]{:S(2)}) collective-permute-start(bf16[528,128]{1,0:T(8,128)(2,1)S(1)} %weighted_sums.5), channel_id=1, source_target_pairs={{448,0},{0,64},{64,128},{128,192},{192,256},{256,320},{320,384},{3... | collective-permute-start | bytes 405512 | tf_op jit(solution)/shard_map/ppermute | solution.py:199
  85.5 1.0 weighted_sums.6
  86.6 0.0 collective-permute-done.4
  86.7 5.1 %collective-permute-start.5 = (bf16[1040,128]{1,0:T(8,128)(2,1)S(1)}, bf16[1040,128]{1,0:T(8,128)(2,1)S(1)}, u32[]{:S(2)}, u32[]{:S(2)}) collective-permute-start(bf16[1040,128]{1,0:T(8,128)(2,1)S(1)} %pad_maximum_fusion.1), channel_id=1, source_target_pairs={{64,0},{128,64},{192,128},{256,192},{320,256},{384,320},{448,384},... | collective-permute-start | bytes 798728 | tf_op jit(solution)/shard_map/ppermute | solution.py:199
  91.8 0.0 collective-permute-done.2
  91.9 1.9 %collective-permute-start.3 = (bf16[1040,128]{1,0:T(8,128)(2,1)S(1)}, bf16[1040,128]{1,0:T(8,128)(2,1)S(1)}, u32[]{:S(2)}, u32[]{:S(2)}) collective-permute-start(bf16[1040,128]{1,0:T(8,128)(2,1)S(1)} %pad_maximum_fusion), channel_id=1, source_target_pairs={{448,0},{0,64},{64,128},{128,192},{192,256},{256,320},{320,384},{3... | collective-permute-start | bytes 798728 | tf_op jit(solution)/shard_map/ppermute | solution.py:199
  93.8 1.0 weighted_sums.8
  94.9 1.2 %collective-permute-done.5 = bf16[1040,128]{1,0:T(8,128)(2,1)S(1)} collective-permute-done((bf16[1040,128]{1,0:T(8,128)(2,1)S(1)}, bf16[1040,128]{1,0:T(8,128)(2,1)S(1)}, u32[]{:S(2)}, u32[]{:S(2)}) %collective-permute-start.5) | collective-permute-done | bytes 266272 | tf_op jit(solution)/shard_map/ppermute | solution.py:199
  96.1 0.1 add_convert_fusion.3
  96.2 5.6 %collective-permute-start.6 = (bf16[1040,128]{1,0:T(8,128)(2,1)S(1)}, bf16[1040,128]{1,0:T(8,128)(2,1)S(1)}, u32[]{:S(2)}, u32[]{:S(2)}) collective-permute-start(bf16[1040,128]{1,0:T(8,128)(2,1)S(1)} %add_convert_fusion.3), channel_id=1, source_target_pairs={{64,0},{128,64},{192,128},{256,192},{320,256},{384,320},{448,384},... | collective-permute-start | bytes 798728 | tf_op jit(solution)/shard_map/ppermute | solution.py:199
  101.8 0.0 collective-permute-done.3
  101.8 0.1 add_convert_fusion.1
  101.9 1.9 %collective-permute-start.8 = (bf16[1040,128]{1,0:T(8,128)(2,1)S(1)}, bf16[1040,128]{1,0:T(8,128)(2,1)S(1)}, u32[]{:S(2)}, u32[]{:S(2)}) collective-permute-start(bf16[1040,128]{1,0:T(8,128)(2,1)S(1)} %add_convert_fusion.1), channel_id=1, source_target_pairs={{448,0},{0,64},{64,128},{128,192},{192,256},{256,320},{320,384},{3... | collective-permute-start | bytes 798728 | tf_op jit(solution)/shard_map/ppermute | solution.py:199
  103.8 1.5 %weighted_sums.7 = (bf16[1040,128]{1,0:T(8,128)(2,1)S(1)}, bf16[1040,128]{1,0:T(8,128)(2,1)S(1)}, bf16[1040,128]{1,0:T(8,128)(2,1)S(1)}) custom-call(s32[1]{0:T(128)} %bitcast.place_ref, f32[32,1536]{1,0:T(8,128)S(1)} %bitcast.24, f32[1024,768]{1,0:T(8,128)S(1)} %get-tuple-element.28.refs_0_, f32[1,768]{1,0:T(1,128)S(1)} %get-tuple-element.29.refs_1_, ...), custom_call_target="tpu_custom_call" | custom-call | flops 1207959552 | bytes 4718592 | tf_op jit(solution)/shard_map/weighted_sums/pallas_call | solution.py:134
  105.3 0.4 collective-permute-done.6
  105.7 0.1 add_convert_fusion.2
  105.8 5.6 %collective-permute-start.7 = (bf16[1040,128]{1,0:T(8,128)(2,1)S(1)}, bf16[1040,128]{1,0:T(8,128)(2,1)S(1)}, u32[]{:S(2)}, u32[]{:S(2)}) collective-permute-start(bf16[1040,128]{1,0:T(8,128)(2,1)S(1)} %add_convert_fusion.2), channel_id=1, source_target_pairs={{64,0},{128,64},{192,128},{256,192},{320,256},{384,320},{448,384},... | collective-permute-start | bytes 798728 | tf_op jit(solution)/shard_map/ppermute | solution.py:199
  111.4 0.0 collective-permute-done.8
  111.4 0.1 add_convert_fusion
  111.5 1.9 %collective-permute-start.9 = (bf16[1040,128]{1,0:T(8,128)(2,1)S(1)}, bf16[1040,128]{1,0:T(8,128)(2,1)S(1)}, u32[]{:S(2)}, u32[]{:S(2)}) collective-permute-start(bf16[1040,128]{1,0:T(8,128)(2,1)S(1)} %add_convert_fusion), channel_id=1, source_target_pairs={{448,0},{0,64},{64,128},{128,192},{192,256},{256,320},{320,384},{3... | collective-permute-start | bytes 798728 | tf_op jit(solution)/shard_map/ppermute | solution.py:199
  113.4 1.9 %collective-permute-done.7.down_ref = bf16[1040,128]{1,0:T(8,128)(2,1)S(1)} collective-permute-done((bf16[1040,128]{1,0:T(8,128)(2,1)S(1)}, bf16[1040,128]{1,0:T(8,128)(2,1)S(1)}, u32[]{:S(2)}, u32[]{:S(2)}) %collective-permute-start.7) | collective-permute-done | bytes 266272 | tf_op jit(solution)/shard_map/ppermute | solution.py:199
  115.3 5.7 %collective-permute-done.9.up_ref = bf16[1040,128]{1,0:T(8,128)(2,1)S(1)} collective-permute-done((bf16[1040,128]{1,0:T(8,128)(2,1)S(1)}, bf16[1040,128]{1,0:T(8,128)(2,1)S(1)}, u32[]{:S(2)}, u32[]{:S(2)}) %collective-permute-start.9) | collective-permute-done | bytes 266272 | tf_op jit(solution)/shard_map/ppermute | solution.py:199
  121.0 0.9 finish.1
  (12 shorter events, 0.2 us)
Async XLA Ops:
  23.1 27.6 %copy-start = (bf16[1024,1024]{1,0:T(8,128)(2,1)S(1)}, bf16[1024,1024]{1,0:T(8,128)(2,1)}, u32[]{:S(2)}) copy-start(bf16[1024,1024]{1,0:T(8,128)(2,1)} %cent_ref.3) | copy-start | bytes 6291460
  48.8 5.3 %collective-permute-start = (bf16[1024,768]{1,0:T(8,128)(2,1)S(1)}, bf16[1024,768]{1,0:T(8,128)(2,1)S(1)}, u32[]{:S(2)}, u32[]{:S(2)}) collective-permute-start(bf16[1024,768]{1,0:T(8,128)(2,1)S(1)} %bitcast.13), channel_id=1, source_target_pairs={{0,1},{1,0},{2,3},{3,2},{4,5},{5,4},{6,7},{7,6},{8,9},{9,8},{10,11... | collective-permute-start | bytes 4718600 | tf_op jit(solution)/shard_map/ppermute | solution.py:179
  56.6 3.1 %collective-permute-start.1 = (f32[1,1536]{1,0:T(1,128)S(1)}, f32[1,1536]{1,0:T(1,128)S(1)}, u32[]{:S(2)}, u32[]{:S(2)}) collective-permute-start(f32[1,1536]{1,0:T(1,128)S(1)} %pad_maximum_fusion.3), channel_id=1, source_target_pairs={{0,1},{1,0},{2,3},{3,2},{4,5},{5,4},{6,7},{7,6},{8,9},{9,8},{10,11... | collective-permute-start | bytes 18440 | tf_op jit(solution)/shard_map/ppermute | solution.py:179
  77.5 9.1 %collective-permute-start.4 = (bf16[512,128]{1,0:T(8,128)(2,1)S(1)}, bf16[512,128]{1,0:T(8,128)(2,1)S(1)}, u32[]{:S(2)}, u32[]{:S(2)}) collective-permute-start(bf16[512,128]{1,0:T(8,128)(2,1)S(1)} %weighted_sums.9), channel_id=1, source_target_pairs={{64,0},{128,64},{192,128},{256,192},{320,256},{384,320},{448,384},... | collective-permute-start | bytes 393224 | tf_op jit(solution)/shard_map/ppermute | solution.py:199
  83.6 8.2 %collective-permute-start.2 = (bf16[528,128]{1,0:T(8,128)(2,1)S(1)}, bf16[528,128]{1,0:T(8,128)(2,1)S(1)}, u32[]{:S(2)}, u32[]{:S(2)}) collective-permute-start(bf16[528,128]{1,0:T(8,128)(2,1)S(1)} %weighted_sums.5), channel_id=1, source_target_pairs={{448,0},{0,64},{64,128},{128,192},{192,256},{256,320},{320,384},{3... | collective-permute-start | bytes 405512 | tf_op jit(solution)/shard_map/ppermute | solution.py:199
  86.7 9.4 %collective-permute-start.5 = (bf16[1040,128]{1,0:T(8,128)(2,1)S(1)}, bf16[1040,128]{1,0:T(8,128)(2,1)S(1)}, u32[]{:S(2)}, u32[]{:S(2)}) collective-permute-start(bf16[1040,128]{1,0:T(8,128)(2,1)S(1)} %pad_maximum_fusion.1), channel_id=1, source_target_pairs={{64,0},{128,64},{192,128},{256,192},{320,256},{384,320},{448,384},... | collective-permute-start | bytes 798728 | tf_op jit(solution)/shard_map/ppermute | solution.py:199
  91.9 9.9 %collective-permute-start.3 = (bf16[1040,128]{1,0:T(8,128)(2,1)S(1)}, bf16[1040,128]{1,0:T(8,128)(2,1)S(1)}, u32[]{:S(2)}, u32[]{:S(2)}) collective-permute-start(bf16[1040,128]{1,0:T(8,128)(2,1)S(1)} %pad_maximum_fusion), channel_id=1, source_target_pairs={{448,0},{0,64},{64,128},{128,192},{192,256},{256,320},{320,384},{3... | collective-permute-start | bytes 798728 | tf_op jit(solution)/shard_map/ppermute | solution.py:199
  96.2 9.5 %collective-permute-start.6 = (bf16[1040,128]{1,0:T(8,128)(2,1)S(1)}, bf16[1040,128]{1,0:T(8,128)(2,1)S(1)}, u32[]{:S(2)}, u32[]{:S(2)}) collective-permute-start(bf16[1040,128]{1,0:T(8,128)(2,1)S(1)} %add_convert_fusion.3), channel_id=1, source_target_pairs={{64,0},{128,64},{192,128},{256,192},{320,256},{384,320},{448,384},... | collective-permute-start | bytes 798728 | tf_op jit(solution)/shard_map/ppermute | solution.py:199
  101.9 9.5 %collective-permute-start.8 = (bf16[1040,128]{1,0:T(8,128)(2,1)S(1)}, bf16[1040,128]{1,0:T(8,128)(2,1)S(1)}, u32[]{:S(2)}, u32[]{:S(2)}) collective-permute-start(bf16[1040,128]{1,0:T(8,128)(2,1)S(1)} %add_convert_fusion.1), channel_id=1, source_target_pairs={{448,0},{0,64},{64,128},{128,192},{192,256},{256,320},{320,384},{3... | collective-permute-start | bytes 798728 | tf_op jit(solution)/shard_map/ppermute | solution.py:199
  105.8 9.5 %collective-permute-start.7 = (bf16[1040,128]{1,0:T(8,128)(2,1)S(1)}, bf16[1040,128]{1,0:T(8,128)(2,1)S(1)}, u32[]{:S(2)}, u32[]{:S(2)}) collective-permute-start(bf16[1040,128]{1,0:T(8,128)(2,1)S(1)} %add_convert_fusion.2), channel_id=1, source_target_pairs={{64,0},{128,64},{192,128},{256,192},{320,256},{384,320},{448,384},... | collective-permute-start | bytes 798728 | tf_op jit(solution)/shard_map/ppermute | solution.py:199
  111.5 9.5 %collective-permute-start.9 = (bf16[1040,128]{1,0:T(8,128)(2,1)S(1)}, bf16[1040,128]{1,0:T(8,128)(2,1)S(1)}, u32[]{:S(2)}, u32[]{:S(2)}) collective-permute-start(bf16[1040,128]{1,0:T(8,128)(2,1)S(1)} %add_convert_fusion), channel_id=1, source_target_pairs={{448,0},{0,64},{64,128},{128,192},{192,256},{256,320},{320,384},{3... | collective-permute-start | bytes 798728 | tf_op jit(solution)/shard_map/ppermute | solution.py:199

commit v7 on v4

--- a/solution.py
+++ b/solution.py
@@ -222,7 +222,7 @@
     starts = 0, far[0].shape[0]
     near = make_near(far[0])
     while len(near) > 1:
-        rest = make_near(up) if len(near) == 2 else near[2:]
+        rest = make_near(up)
         down = dp_shift(add(near[0], down, starts[0]), 1)
         up = dp_shift(add(near[1], up, starts[1]), -1)
         near = rest
@@ -245,7 +245,7 @@
     halves = ((raised_0, peak_0, mine), (raised_1, peak_1, other))
     order = ring_order(n_dp)
     far = weighted_sums(order[:1], n_dp, True, place, lse, halves)
-    rounds = [order[i:i + 2] for i in range(1, n_dp - 3, 2)] + [order[-3:]]
+    rounds = [order[i:i + 2] for i in range(1, n_dp - 1, 2)] + [order[-1:]]
 
     def make_near(after):
         late, _ = lax.optimization_barrier((lse, after))

time: 122 us -> 122 us (level)
    pallas_call x4 -> x5, Pallas kernels: 4.71 us -> 5.44 us  [weighted_sums(): pl.pallas_call(functools.partial(sums_kernel, order, n_blocks), out_shape...]
  transfers between devices with their start and end apart: 10 -> 10, of which waited for: 6 -> 6; matrix products, arithmetic and copies ran while one was open for 0% -> 0% of each run, Pallas kernels for 5% -> 6%
where the time goes in v7:
time: 122 us
  blocking collectives  64.3 us (53%)
  starting transfers between devices  33.3 us (27%)
  Pallas kernels  11.5 us (9%)
  waiting for transfers between devices  10.2 us (8%)
    all_to_all x2, blocking collectives, spread(): lax.all_to_all(jnp.broadcast_to(value[None], (n,) + value.shape), axis, 0...  42.6 us
    ppermute x8, starting transfers between devices, dp_shift(): return lax.ppermute(value, 'dp', [((i + d) % n, i) for i in range(n)])  29.4 us
    all_to_all x1, blocking collectives, gather_half(): lax.all_to_all(blocks, ('z', 'core'), 0, 0).reshape(-1, n_tok // n_core)  21.7 us
    ppermute x8, waiting for transfers between devices, dp_shift(): return lax.ppermute(value, 'dp', [((i + d) % n, i) for i in range(n)])  8.54 us
    pallas_call x5, Pallas kernels, weighted_sums(): pl.pallas_call(functools.partial(sums_kernel, order, n_blocks), out_shape...  5.44 us
    pallas_call x2, Pallas kernels, local_softmax(): pl.pallas_call(norms_kernel if norms is None else logits_kernel, out_shap...  5.16 us
    ppermute x2, starting transfers between devices, core_swap(): return lax.ppermute(value, 'core', [(0, 1), (1, 0)])  3.95 us
  transfers between devices with their start and end apart: 10, of which 6 were waited for; matrix products, arithmetic and copies ran while one was open for 0% of the time, Pallas kernels for 6%

profile of v7, /device:TPU:64, one launch (start us, length us, event | category | flops | bytes accessed | tf_op | source)
XLA Modules:
  0.0 121.7 jit_solution(15779211859075049273)
XLA Ops:
  0.6 0.8 slice_bitcast_fusion.1
  1.4 21.7 %all_to_all.18 = bf16[16,16,768]{2,1,0:T(8,128)(2,1)S(1)} all-to-all(bf16[16,16,768]{2,1,0:T(8,128)(2,1)S(1)} %bitcast.25), channel_id=1, replica_groups=mesh['dp'=8,'x'=4,'z'=8,'core'=2] {'z','core'}, dimensions={0} | all-to-all | bytes 786432 | tf_op jit(solution)/shard_map/all_to_all | solution.py:199
  23.1 0.0 copy-start
  23.1 0.1 broadcast_in_dim.20
  23.2 25.6 %all_to_all.19 = bf16[4,256,768]{2,1,0:T(8,128)(2,1)S(1)} all-to-all(bf16[4,256,768]{2,1,0:T(8,128)(2,1)S(1)} %broadcast_in_dim.20), channel_id=1, replica_groups=mesh['dp'=8,'x'=4,'z'=8,'core'=2] {'x'}, dimensions={0} | all-to-all | bytes 3145728 | tf_op jit(solution)/shard_map/all_to_all | solution.py:190
  48.8 1.9 %collective-permute-start = (bf16[1024,768]{1,0:T(8,128)(2,1)S(1)}, bf16[1024,768]{1,0:T(8,128)(2,1)S(1)}, u32[]{:S(2)}, u32[]{:S(2)}) collective-permute-start(bf16[1024,768]{1,0:T(8,128)(2,1)S(1)} %bitcast.13), channel_id=1, source_target_pairs={{0,1},{1,0},{2,3},{3,2},{4,5},{5,4},{6,7},{7,6},{8,9},{9,8},{10,11... | collective-permute-start | bytes 4718600 | tf_op jit(solution)/shard_map/ppermute | solution.py:185
  50.7 0.0 copy-done
  50.7 2.7 %local_softmax.2 = (f32[1024,768]{1,0:T(8,128)S(1)}, f32[1,768]{1,0:T(1,128)S(1)}, f32[1,768]{1,0:T(1,128)S(1)}, f32[1024,128]{1,0:T(8,128)S(1)}) custom-call(bf16[1024,1024]{1,0:T(8,128)(2,1)S(1)} %copy-done, bf16[1024,768]{1,0:T(8,128)(2,1)S(1)} %bitcast.14), custom_call_target="tpu_custom_call" | custom-call | flops 1610612736 | bytes 6291456 | tf_op jit(solution)/shard_map/local_softmax/pallas_call | solution.py:69
  53.5 0.6 collective-permute-done.points_ref.refs_5_
  54.1 2.5 %local_softmax.3 = (f32[1024,768]{1,0:T(8,128)S(1)}, f32[1,768]{1,0:T(1,128)S(1)}, f32[1,768]{1,0:T(1,128)S(1)}) custom-call(bf16[1024,1024]{1,0:T(8,128)(2,1)S(1)} %copy-done, bf16[1024,768]{1,0:T(8,128)(2,1)S(1)} %collective-permute-done.points_ref.refs_5_, f32[1024,128]{1,0:T(8,128)S(1)} %get-tuple-element.28.norm_ref), custom_call_target="tpu_custom_call" | custom-call | flops 1610612736 | bytes 6291456 | tf_op jit(solution)/shard_map/local_softmax/pallas_call | solution.py:69
  56.6 2.0 %collective-permute-start.1 = (f32[1,1536]{1,0:T(1,128)S(1)}, f32[1,1536]{1,0:T(1,128)S(1)}, u32[]{:S(2)}, u32[]{:S(2)}) collective-permute-start(f32[1,1536]{1,0:T(1,128)S(1)} %pad_maximum_fusion.3), channel_id=1, source_target_pairs={{0,1},{1,0},{2,3},{3,2},{4,5},{5,4},{6,7},{7,6},{8,9},{9,8},{10,11... | collective-permute-start | bytes 18440 | tf_op jit(solution)/shard_map/ppermute | solution.py:185
  58.6 1.0 collective-permute-done.1
  59.6 0.1 fusion
  59.7 0.1 broadcast_in_dim.21
  59.8 17.0 %all_to_all.20 = f32[32,1,1536]{2,1,0:T(1,128)S(1)} all-to-all(f32[32,1,1536]{2,1,0:T(1,128)S(1)} %broadcast_in_dim.21), channel_id=1, replica_groups=mesh['dp'=8,'x'=4,'z'=8,'core'=2] {'x','z'}, dimensions={0} | all-to-all | bytes 393216 | tf_op jit(solution)/shard_map/all_to_all | solution.py:190
  76.8 1.2 weighted_sums.5
  78.0 5.4 %collective-permute-start.5 = (bf16[512,128]{1,0:T(8,128)(2,1)S(1)}, bf16[512,128]{1,0:T(8,128)(2,1)S(1)}, u32[]{:S(2)}, u32[]{:S(2)}) collective-permute-start(bf16[512,128]{1,0:T(8,128)(2,1)S(1)} %get-tuple-element.37), channel_id=1, source_target_pairs={{64,0},{128,64},{192,128},{256,192},{320,256},{384,320},{448,384},... | collective-permute-start | bytes 393224 | tf_op jit(solution)/shard_map/ppermute | solution.py:205
  83.4 1.9 %collective-permute-start.2 = (bf16[528,128]{1,0:T(8,128)(2,1)S(1)}, bf16[528,128]{1,0:T(8,128)(2,1)S(1)}, u32[]{:S(2)}, u32[]{:S(2)}) collective-permute-start(bf16[528,128]{1,0:T(8,128)(2,1)S(1)} %get-tuple-element.34), channel_id=1, source_target_pairs={{448,0},{0,64},{64,128},{128,192},{192,256},{256,320},{320,384},{3... | collective-permute-start | bytes 405512 | tf_op jit(solution)/shard_map/ppermute | solution.py:205
  85.3 1.0 weighted_sums.7
  86.4 0.0 collective-permute-done.5
  86.5 5.1 %collective-permute-start.6 = (bf16[1040,128]{1,0:T(8,128)(2,1)S(1)}, bf16[1040,128]{1,0:T(8,128)(2,1)S(1)}, u32[]{:S(2)}, u32[]{:S(2)}) collective-permute-start(bf16[1040,128]{1,0:T(8,128)(2,1)S(1)} %pad_maximum_fusion.1), channel_id=1, source_target_pairs={{64,0},{128,64},{192,128},{256,192},{320,256},{384,320},{448,384},... | collective-permute-start | bytes 798728 | tf_op jit(solution)/shard_map/ppermute | solution.py:205
  91.6 0.0 collective-permute-done.2
  91.7 1.9 %collective-permute-start.3 = (bf16[1040,128]{1,0:T(8,128)(2,1)S(1)}, bf16[1040,128]{1,0:T(8,128)(2,1)S(1)}, u32[]{:S(2)}, u32[]{:S(2)}) collective-permute-start(bf16[1040,128]{1,0:T(8,128)(2,1)S(1)} %pad_maximum_fusion), channel_id=1, source_target_pairs={{448,0},{0,64},{64,128},{128,192},{192,256},{256,320},{320,384},{3... | collective-permute-start | bytes 798728 | tf_op jit(solution)/shard_map/ppermute | solution.py:205
  93.6 1.0 weighted_sums.6
  94.7 1.2 %collective-permute-done.6 = bf16[1040,128]{1,0:T(8,128)(2,1)S(1)} collective-permute-done((bf16[1040,128]{1,0:T(8,128)(2,1)S(1)}, bf16[1040,128]{1,0:T(8,128)(2,1)S(1)}, u32[]{:S(2)}, u32[]{:S(2)}) %collective-permute-start.6) | collective-permute-done | bytes 266272 | tf_op jit(solution)/shard_map/ppermute | solution.py:205
  95.9 0.1 add_convert_fusion.2
  96.0 5.6 %collective-permute-start.7 = (bf16[1040,128]{1,0:T(8,128)(2,1)S(1)}, bf16[1040,128]{1,0:T(8,128)(2,1)S(1)}, u32[]{:S(2)}, u32[]{:S(2)}) collective-permute-start(bf16[1040,128]{1,0:T(8,128)(2,1)S(1)} %add_convert_fusion.2), channel_id=1, source_target_pairs={{64,0},{128,64},{192,128},{256,192},{320,256},{384,320},{448,384},... | collective-permute-start | bytes 798728 | tf_op jit(solution)/shard_map/ppermute | solution.py:205
  101.6 0.0 collective-permute-done.3
  101.6 0.1 add_convert_fusion.3
  101.7 1.9 %collective-permute-start.4 = (bf16[1040,128]{1,0:T(8,128)(2,1)S(1)}, bf16[1040,128]{1,0:T(8,128)(2,1)S(1)}, u32[]{:S(2)}, u32[]{:S(2)}) collective-permute-start(bf16[1040,128]{1,0:T(8,128)(2,1)S(1)} %add_convert_fusion.3), channel_id=1, source_target_pairs={{448,0},{0,64},{64,128},{128,192},{192,256},{256,320},{320,384},{3... | collective-permute-start | bytes 798728 | tf_op jit(solution)/shard_map/ppermute | solution.py:205
  103.6 1.0 weighted_sums.9
  104.7 0.8 collective-permute-done.7
  105.5 0.1 add_convert_fusion.1
  105.6 5.6 %collective-permute-start.8 = (bf16[1040,128]{1,0:T(8,128)(2,1)S(1)}, bf16[1040,128]{1,0:T(8,128)(2,1)S(1)}, u32[]{:S(2)}, u32[]{:S(2)}) collective-permute-start(bf16[1040,128]{1,0:T(8,128)(2,1)S(1)} %add_convert_fusion.1), channel_id=1, source_target_pairs={{64,0},{128,64},{192,128},{256,192},{320,256},{384,320},{448,384},... | collective-permute-start | bytes 798728 | tf_op jit(solution)/shard_map/ppermute | solution.py:205
  111.2 0.0 collective-permute-done.4
  111.2 0.1 add_convert_fusion
  111.3 1.9 %collective-permute-start.9 = (bf16[1040,128]{1,0:T(8,128)(2,1)S(1)}, bf16[1040,128]{1,0:T(8,128)(2,1)S(1)}, u32[]{:S(2)}, u32[]{:S(2)}) collective-permute-start(bf16[1040,128]{1,0:T(8,128)(2,1)S(1)} %add_convert_fusion), channel_id=1, source_target_pairs={{448,0},{0,64},{64,128},{128,192},{192,256},{256,320},{320,384},{3... | collective-permute-start | bytes 798728 | tf_op jit(solution)/shard_map/ppermute | solution.py:205
  113.2 1.2 weighted_sums.8.own_ref
  114.4 0.7 collective-permute-done.8.down_ref
  115.1 5.7 %collective-permute-done.9.up_ref = bf16[1040,128]{1,0:T(8,128)(2,1)S(1)} collective-permute-done((bf16[1040,128]{1,0:T(8,128)(2,1)S(1)}, bf16[1040,128]{1,0:T(8,128)(2,1)S(1)}, u32[]{:S(2)}, u32[]{:S(2)}) %collective-permute-start.9) | collective-permute-done | bytes 266272 | tf_op jit(solution)/shard_map/ppermute | solution.py:205
  120.8 0.9 finish.1
  (12 shorter events, 0.2 us)
Async XLA Ops:
  23.1 27.6 %copy-start = (bf16[1024,1024]{1,0:T(8,128)(2,1)S(1)}, bf16[1024,1024]{1,0:T(8,128)(2,1)}, u32[]{:S(2)}) copy-start(bf16[1024,1024]{1,0:T(8,128)(2,1)} %cent_ref.3) | copy-start | bytes 6291460
  48.8 5.3 %collective-permute-start = (bf16[1024,768]{1,0:T(8,128)(2,1)S(1)}, bf16[1024,768]{1,0:T(8,128)(2,1)S(1)}, u32[]{:S(2)}, u32[]{:S(2)}) collective-permute-start(bf16[1024,768]{1,0:T(8,128)(2,1)S(1)} %bitcast.13), channel_id=1, source_target_pairs={{0,1},{1,0},{2,3},{3,2},{4,5},{5,4},{6,7},{7,6},{8,9},{9,8},{10,11... | collective-permute-start | bytes 4718600 | tf_op jit(solution)/shard_map/ppermute | solution.py:185
  56.6 3.1 %collective-permute-start.1 = (f32[1,1536]{1,0:T(1,128)S(1)}, f32[1,1536]{1,0:T(1,128)S(1)}, u32[]{:S(2)}, u32[]{:S(2)}) collective-permute-start(f32[1,1536]{1,0:T(1,128)S(1)} %pad_maximum_fusion.3), channel_id=1, source_target_pairs={{0,1},{1,0},{2,3},{3,2},{4,5},{5,4},{6,7},{7,6},{8,9},{9,8},{10,11... | collective-permute-start | bytes 18440 | tf_op jit(solution)/shard_map/ppermute | solution.py:185
  78.0 8.4 %collective-permute-start.5 = (bf16[512,128]{1,0:T(8,128)(2,1)S(1)}, bf16[512,128]{1,0:T(8,128)(2,1)S(1)}, u32[]{:S(2)}, u32[]{:S(2)}) collective-permute-start(bf16[512,128]{1,0:T(8,128)(2,1)S(1)} %get-tuple-element.37), channel_id=1, source_target_pairs={{64,0},{128,64},{192,128},{256,192},{320,256},{384,320},{448,384},... | collective-permute-start | bytes 393224 | tf_op jit(solution)/shard_map/ppermute | solution.py:205
  83.4 8.2 %collective-permute-start.2 = (bf16[528,128]{1,0:T(8,128)(2,1)S(1)}, bf16[528,128]{1,0:T(8,128)(2,1)S(1)}, u32[]{:S(2)}, u32[]{:S(2)}) collective-permute-start(bf16[528,128]{1,0:T(8,128)(2,1)S(1)} %get-tuple-element.34), channel_id=1, source_target_pairs={{448,0},{0,64},{64,128},{128,192},{192,256},{256,320},{320,384},{3... | collective-permute-start | bytes 405512 | tf_op jit(solution)/shard_map/ppermute | solution.py:205
  86.5 9.4 %collective-permute-start.6 = (bf16[1040,128]{1,0:T(8,128)(2,1)S(1)}, bf16[1040,128]{1,0:T(8,128)(2,1)S(1)}, u32[]{:S(2)}, u32[]{:S(2)}) collective-permute-start(bf16[1040,128]{1,0:T(8,128)(2,1)S(1)} %pad_maximum_fusion.1), channel_id=1, source_target_pairs={{64,0},{128,64},{192,128},{256,192},{320,256},{384,320},{448,384},... | collective-permute-start | bytes 798728 | tf_op jit(solution)/shard_map/ppermute | solution.py:205
  91.7 9.9 %collective-permute-start.3 = (bf16[1040,128]{1,0:T(8,128)(2,1)S(1)}, bf16[1040,128]{1,0:T(8,128)(2,1)S(1)}, u32[]{:S(2)}, u32[]{:S(2)}) collective-permute-start(bf16[1040,128]{1,0:T(8,128)(2,1)S(1)} %pad_maximum_fusion), channel_id=1, source_target_pairs={{448,0},{0,64},{64,128},{128,192},{192,256},{256,320},{320,384},{3... | collective-permute-start | bytes 798728 | tf_op jit(solution)/shard_map/ppermute | solution.py:205
  96.0 9.5 %collective-permute-start.7 = (bf16[1040,128]{1,0:T(8,128)(2,1)S(1)}, bf16[1040,128]{1,0:T(8,128)(2,1)S(1)}, u32[]{:S(2)}, u32[]{:S(2)}) collective-permute-start(bf16[1040,128]{1,0:T(8,128)(2,1)S(1)} %add_convert_fusion.2), channel_id=1, source_target_pairs={{64,0},{128,64},{192,128},{256,192},{320,256},{384,320},{448,384},... | collective-permute-start | bytes 798728 | tf_op jit(solution)/shard_map/ppermute | solution.py:205
  101.7 9.5 %collective-permute-start.4 = (bf16[1040,128]{1,0:T(8,128)(2,1)S(1)}, bf16[1040,128]{1,0:T(8,128)(2,1)S(1)}, u32[]{:S(2)}, u32[]{:S(2)}) collective-permute-start(bf16[1040,128]{1,0:T(8,128)(2,1)S(1)} %add_convert_fusion.3), channel_id=1, source_target_pairs={{448,0},{0,64},{64,128},{128,192},{192,256},{256,320},{320,384},{3... | collective-permute-start | bytes 798728 | tf_op jit(solution)/shard_map/ppermute | solution.py:205
  105.6 9.5 %collective-permute-start.8 = (bf16[1040,128]{1,0:T(8,128)(2,1)S(1)}, bf16[1040,128]{1,0:T(8,128)(2,1)S(1)}, u32[]{:S(2)}, u32[]{:S(2)}) collective-permute-start(bf16[1040,128]{1,0:T(8,128)(2,1)S(1)} %add_convert_fusion.1), channel_id=1, source_target_pairs={{64,0},{128,64},{192,128},{256,192},{320,256},{384,320},{448,384},... | collective-permute-start | bytes 798728 | tf_op jit(solution)/shard_map/ppermute | solution.py:205
  111.3 9.5 %collective-permute-start.9 = (bf16[1040,128]{1,0:T(8,128)(2,1)S(1)}, bf16[1040,128]{1,0:T(8,128)(2,1)S(1)}, u32[]{:S(2)}, u32[]{:S(2)}) collective-permute-start(bf16[1040,128]{1,0:T(8,128)(2,1)S(1)} %add_convert_fusion), channel_id=1, source_target_pairs={{448,0},{0,64},{64,128},{128,192},{192,256},{256,320},{320,384},{3... | collective-permute-start | bytes 798728 | tf_op jit(solution)/shard_map/ppermute | solution.py:205
